TPU v7x, 256 devices: a whole 4x4x8 slice. The times are simulated.
256 devices in a mesh: cell: 32 (over z, y), view: 8 (over x, core).
Axes of the slice: x: 4, y: 4, z: 8, core: 2. Of those that a mesh axis runs over, the one named last changes fastest.
Arguments:
- gaussians: float32 [59, 1048576], P(None, 'cell'), may hold values from -256 to 256
- cameras: float32 [8, 7], P('view'), may hold values from -1 to 1.005
- fetch_ids: int32 [32, 32, 128], P('cell'), may hold values from 0 to 32767, as said below
- tile_lists: int32 [8, 256, 512], P('view', 'cell'), may hold values from 0 to 4095, as said below
- lengths: int32 [256], P('cell'), may hold values from 128 to 512, as said below
- target_image: float32 [3, 8, 256, 256], P(None, 'view', 'cell'), may hold values from 0 to 1
Outputs:
- rendered: float32 [3, 8, 256, 256], P(None, 'view', 'cell')
- param_grads: float32 [59, 1048576], P(None, ('cell', 'view'))
Inputs may be any that keep to these rules, and one draw needn't show every extreme that they name: Each row fetch_ids[c, o] holds 128 distinct local indices of owner cell o, and no index stands under two requesting cells. `tile_lists`: A value o * 128 + s names slot s of owner cell o in the fetch_ids row of the tile's cell (t // 8). The first lengths[t] entries of a tile are distinct; the rest are ignored. `lengths`: on every index of cell some tile has 512 live entries.
All inputs are finite; a program needn't handle non-finite values.
Results may differ from a plain program's by a relative error of at most 0.0003.
Values sent between devices are 32-bit elements; how exact they have to be, the bound alone decides.
A program may use at most 128 MiB of HBM per device.

v0:
```python
import jax
import jax.numpy as jnp
from jax import lax
from jax.sharding import PartitionSpec as P

harmonic_zero = 0.28209479177387814
harmonic_one = 0.4886025119029199
harmonic_two = (
    1.0925484305920792,
    -1.0925484305920792,
    0.31539156525252005,
    -1.0925484305920792,
    0.5462742152960396,
)
harmonic_three = (
    -0.5900435899266435,
    2.890611442640554,
    -0.4570457994644658,
    0.3731763325901154,
    -0.4570457994644658,
    1.445305721320277,
    -0.5900435899266435,
)


def harmonic_basis(direction):
    along_x, along_y, along_z = (direction[0], direction[1], direction[2])
    square_x, square_y, square_z = (along_x * along_x, along_y * along_y, along_z * along_z)
    terms = [
        harmonic_zero + 0.0 * along_x,
        -harmonic_one * along_y,
        harmonic_one * along_z,
        -harmonic_one * along_x,
        harmonic_two[0] * along_x * along_y,
        harmonic_two[1] * along_y * along_z,
        harmonic_two[2] * (2.0 * square_z - square_x - square_y),
        harmonic_two[3] * along_x * along_z,
        harmonic_two[4] * (square_x - square_y),
        harmonic_three[0] * along_y * (3.0 * square_x - square_y),
        harmonic_three[1] * along_x * along_y * along_z,
        harmonic_three[2] * along_y * (4.0 * square_z - square_x - square_y),
        harmonic_three[3] * along_z * (2.0 * square_z - 3.0 * square_x - 3.0 * square_y),
        harmonic_three[4] * along_x * (4.0 * square_z - square_x - square_y),
        harmonic_three[5] * along_z * (square_x - square_y),
        harmonic_three[6] * along_x * (square_x - 3.0 * square_y),
    ]
    return jnp.stack(terms)


def camera_rotation(camera):
    cos_yaw, sin_yaw = (jnp.cos(camera[0]), jnp.sin(camera[0]))
    cos_pitch, sin_pitch = (jnp.cos(camera[1]), jnp.sin(camera[1]))
    cos_roll, sin_roll = (jnp.cos(camera[2]), jnp.sin(camera[2]))
    return [
        [
            cos_yaw * cos_pitch,
            cos_yaw * sin_pitch * sin_roll - sin_yaw * cos_roll,
            cos_yaw * sin_pitch * cos_roll + sin_yaw * sin_roll,
        ],
        [
            sin_yaw * cos_pitch,
            sin_yaw * sin_pitch * sin_roll + cos_yaw * cos_roll,
            sin_yaw * sin_pitch * cos_roll - cos_yaw * sin_roll,
        ],
        [-sin_pitch, cos_pitch * sin_roll, cos_pitch * cos_roll],
    ]


def project(values, camera, height):
    rotation = camera_rotation(camera)
    position = values[0:3]
    across = (
        rotation[0][0] * position[0] + rotation[0][1] * position[1] + rotation[0][2] * position[2]
    )
    upward = (
        rotation[1][0] * position[0] + rotation[1][1] * position[1] + rotation[1][2] * position[2]
    )
    screen_u = camera[5] * across + 64.0 + camera[3]
    screen_v = camera[6] * upward + 0.5 * height + camera[4]
    scales = jnp.exp(values[3:6])
    quaternion = values[6:10]
    magnitude = jnp.maximum(jnp.sqrt(jnp.sum(quaternion * quaternion, axis=0)), 0.5)
    real_part = quaternion[0] / magnitude
    imag_x = quaternion[1] / magnitude
    imag_y = quaternion[2] / magnitude
    imag_z = quaternion[3] / magnitude
    turned = [
        [
            1.0 - 2.0 * (imag_y * imag_y + imag_z * imag_z),
            2.0 * (imag_x * imag_y - real_part * imag_z),
            2.0 * (imag_x * imag_z + real_part * imag_y),
        ],
        [
            2.0 * (imag_x * imag_y + real_part * imag_z),
            1.0 - 2.0 * (imag_x * imag_x + imag_z * imag_z),
            2.0 * (imag_y * imag_z - real_part * imag_x),
        ],
        [
            2.0 * (imag_x * imag_z - real_part * imag_y),
            2.0 * (imag_y * imag_z + real_part * imag_x),
            1.0 - 2.0 * (imag_x * imag_x + imag_y * imag_y),
        ],
    ]
    first_row = [
        camera[5]
        * (
            rotation[0][0] * turned[0][col]
            + rotation[0][1] * turned[1][col]
            + rotation[0][2] * turned[2][col]
        )
        * scales[col]
        for col in range(3)
    ]
    second_row = [
        camera[6]
        * (
            rotation[1][0] * turned[0][col]
            + rotation[1][1] * turned[1][col]
            + rotation[1][2] * turned[2][col]
        )
        * scales[col]
        for col in range(3)
    ]
    sigma_uu = (
        first_row[0] * first_row[0]
        + first_row[1] * first_row[1]
        + first_row[2] * first_row[2]
        + 0.3
    )
    sigma_uv = (
        first_row[0] * second_row[0] + first_row[1] * second_row[1] + first_row[2] * second_row[2]
    )
    sigma_vv = (
        second_row[0] * second_row[0]
        + second_row[1] * second_row[1]
        + second_row[2] * second_row[2]
        + 0.3
    )
    determinant = sigma_uu * sigma_vv - sigma_uv * sigma_uv
    opacity = jax.nn.sigmoid(values[10])
    harmonics = harmonic_basis(jnp.stack(rotation[2]))
    coefficients = values[11:59].reshape(16, 3, values.shape[1])
    colors = 0.5 + jnp.sum(harmonics[:, None, None] * coefficients, axis=0)
    return jnp.stack(
        [
            screen_u,
            screen_v,
            sigma_vv / determinant,
            -sigma_uv / determinant,
            sigma_uu / determinant,
            opacity,
            colors[0],
            colors[1],
            colors[2],
        ]
    )


def render(features, live_count, tile_index):
    list_len = features.shape[1]
    pixel_index = jnp.arange(256, dtype=jnp.int32)
    pixel_u = (tile_index % 8 * 16 + pixel_index % 16).astype(jnp.float32) + 0.5
    pixel_v = (tile_index // 8 * 16 + pixel_index // 16).astype(jnp.float32) + 0.5
    offset_u = pixel_u[None, :] - features[0][:, None]
    offset_v = pixel_v[None, :] - features[1][:, None]
    power = -0.5 * (
        features[2][:, None] * offset_u * offset_u
        + 2.0 * features[3][:, None] * offset_u * offset_v
        + features[4][:, None] * offset_v * offset_v
    )
    active = (jnp.arange(list_len, dtype=jnp.int32) < live_count)[:, None]
    alpha = jnp.where(active, jnp.minimum(features[5][:, None] * jnp.exp(power), 0.99), 0.0)
    log_keep = jnp.log(1.0 - alpha)
    before = jnp.cumsum(log_keep, axis=0) - log_keep
    weight = jnp.exp(before) * alpha
    return jnp.dot(features[6:9], weight, precision=lax.Precision.HIGHEST)


def on_device(gaussians, cameras, fetch_ids, tile_lists, lengths, target_image):
    tiles_dev = tile_lists.shape[1]
    list_len = tile_lists.shape[2]
    cell_count = lax.axis_size("cell")
    height = 2.0 * tiles_dev * cell_count
    camera = cameras[0]
    tile_ids = lax.axis_index("cell") * tiles_dev + jnp.arange(tiles_dev, dtype=jnp.int32)
    requests = fetch_ids[0]
    wanted = lax.all_to_all(requests, "cell", split_axis=0, concat_axis=0, tiled=True)
    flat_ids = wanted.reshape(-1)
    columns = jnp.take(gaussians, flat_ids, axis=1)
    payload = columns
    payload = payload.reshape(payload.shape[0], wanted.shape[0], wanted.shape[1])
    delivered = lax.all_to_all(payload, "cell", split_axis=1, concat_axis=1, tiled=True)
    held_ids = wanted[None]
    width = delivered.shape[0]
    slot_table = delivered.reshape(width, -1)
    picked = tile_lists[0].reshape(-1)
    goal_pixels = jnp.transpose(target_image[:, 0], (1, 0, 2))

    def total_loss(table_values):
        feature_table = project(table_values, camera, height)
        gathered = jnp.take(feature_table, picked, axis=1).reshape(9, tiles_dev, list_len)
        gathered = jnp.transpose(gathered, (1, 0, 2))
        images = jax.vmap(render)(gathered, lengths, tile_ids)
        return (0.5 * jnp.sum((images - goal_pixels) ** 2), images)

    loss_value, pull_back, images = jax.vjp(total_loss, slot_table, has_aux=True)
    slot_grads = pull_back(jnp.ones((), jnp.float32))[0]
    grad_rows = slot_grads.reshape(width, cell_count, -1)
    returned = lax.all_to_all(grad_rows, "cell", split_axis=1, concat_axis=1, tiled=True)
    held_flat = held_ids.reshape(-1)
    param_count = gaussians.shape[0]
    summed = (
        jnp.zeros(gaussians.shape, jnp.float32)
        .at[:, held_flat]
        .add(returned.reshape(param_count, -1))
    )
    param_grads = lax.psum_scatter(summed, "view", scatter_dimension=1, tiled=True)
    rendered = jnp.transpose(images, (1, 0, 2))[:, None]
    return (rendered, param_grads)


def solution(mesh):
    in_specs = (
        P(None, "cell"),
        P("view", None),
        P("cell", None, None),
        P("view", "cell", None),
        P("cell"),
        P(None, "view", "cell", None),
    )
    out_specs = (P(None, "view", "cell", None), P(None, ("cell", "view")))
    return jax.shard_map(
        on_device, mesh=mesh, in_specs=in_specs, out_specs=out_specs, check_vma=False
    )
```

profile of v0, /device:TPU:1, one launch (start us, length us, event | category | flops | bytes accessed | tf_op | source)
XLA Modules:
  0.0 408.3 jit_solution(12587187095565888392)
XLA Ops:
  7.2 12.0 %all-to-all-start = ((s32[32,1,128]{2,1,0:T(1,128)}), s32[32,1,128]{2,1,0:T(1,128)S(1)}, u32[]{:S(2)}, u32[]{:S(2)}) async-start(s32[32,1,128]{2,1,0:T(1,128)} %bitcast.298), calls=%async_computation | async-start | bytes 32768 | tf_op jit(solution)/shard_map/all_to_all | solution.py:187
  28.5 12.4 %copy.300 = f32[59,32768]{0,1:T(8,128)} copy(f32[59,32768]{1,0:T(8,128)} %param.6) | data formatting | bytes 15466496 | tf_op args[0]
  41.6 16.5 %gather_fusion = f32[4096,59]{1,0:T(8,128)S(1)} fusion(f32[59,32768]{0,1:T(8,128)} %copy.300, s32[4096]{0:T(1024)S(1)} %broadcast_clamp_fusion.1), kind=kCustom, calls=%fused_computation | custom fusion | bytes 1949696 | tf_op jit(solution)/shard_map/jit(_take)/gather | solution.py:189
  59.9 9.2 %all-to-all-start.1 = ((f32[59,32,128]{2,0,1:T(8,128)}), f32[59,32,128]{2,0,1:T(8,128)S(1)}, u32[]{:S(2)}, u32[]{:S(2)}) async-start(f32[59,32,128]{2,0,1:T(8,128)} %broadcast_select_fusion), calls=%async_computation.1 | async-start | bytes 2097152 | tf_op jit(solution)/shard_map/all_to_all | solution.py:192
  72.4 22.4 %all-to-all-done.1 = f32[59,32,128]{2,0,1:T(8,128)S(1)} async-done(((f32[59,32,128]{2,0,1:T(8,128)}), f32[59,32,128]{2,0,1:T(8,128)S(1)}, u32[]{:S(2)}, u32[]{:S(2)}) %all-to-all-start.1) | async-done | bytes 966688 | tf_op jit(solution)/shard_map/all_to_all | solution.py:192
  97.4 2.4 fusion.126
  99.8 2.6 add_add_fusion.17
  103.5 15.6 %gather_fusion.1 = f32[4096,9]{1,0:T(8,128)} fusion(f32[9,4096]{0,1:T(8,128)S(1)} %copy.312, s32[4096]{0:T(1024)} %broadcast_clamp_fusion), kind=kCustom, calls=%fused_computation.1 | custom fusion | bytes 311296 | tf_op jit(solution)/shard_map/jvp(jit(_take))/gather | solution.py:201
  122.3 3.9 fusion.20
  127.9 5.1 %fusion.46 = f32[8,512,256]{2,1,0:T(8,128)S(1)} fusion(f32[8,256,4,128]{1,3,2,0:T(8,128)S(1)} %copy.321, f32[8,512]{1,0:T(8,128)S(1)} %get-tuple-element.122, f32[8,512]{1,0:T(8,128)S(1)} %get-tuple-element.123, f32[8,256]{1,0:T(8,128)S(1)} %copy-done.15, f32[8,512]{1,0:T(8,128)S(1)} %get-tuple-element.124, f32[8,512]{1,0:T(8,128)S(1)} %get-tuple-element.125, ...), kind=kLoop, calls=%fused_computation.79 | loop fusion | flops 17825792 | bytes 8507392 | tf_op jit(solution)/shard_map/jvp(vmap())/mul | solution.py:175
  135.1 3.6 fusion.118
  138.7 8.9 %fusion.42 = (f32[8,256,512]{1,2,0:T(8,128)S(1)}, f32[8,512,256]{2,1,0:T(8,128)S(1)}) fusion(f32[8,256,4,128]{1,3,2,0:T(8,128)S(1)} %copy.321, f32[8,512]{1,0:T(8,128)S(1)} %get-tuple-element.122, f32[8,512]{1,0:T(8,128)S(1)} %get-tuple-element.123, f32[8,256]{1,0:T(8,128)S(1)} %copy-done.15, f32[8,512]{1,0:T(8,128)S(1)} %get-tuple-element.124, ...), kind=kOutput, calls=%fused_computation.71 | convolution fusion | flops 56629248 | bytes 12824576 | tf_op jit(solution)/shard_map/transpose(jvp(vmap()))/dot_general | solution.py:176
  147.6 10.1 %fusion.44 = f32[8,256,4,128]{1,0,3,2:T(8,128)S(1)} fusion(f32[8,256,4,128]{1,3,2,0:T(8,128)S(1)} %bitcast.252), kind=kOutput, calls=%fused_computation.74 | output fusion | flops 133169152 | bytes 8388608 | tf_op jit(solution)/shard_map/reduce-window.2
  159.4 14.9 %fusion.33 = (f32[8,512]{1,0:T(8,128)S(1)}, f32[8,512]{1,0:T(8,128)S(1)}, f32[8,512]{1,0:T(8,128)S(1)}, f32[8,512]{1,0:T(8,128)S(1)}, f32[8,512]{1,0:T(8,128)S(1)}, /*index=5*/f32[8,512]{1,0:T(8,128)S(1)}) fusion(f32[8,512]{1,0:T(8,128)S(1)} %get-tuple-element.123, f32[8,256]{1,0:T(8,128)S(1)} %copy-done.15, f32[8,512]{1,0:T(8,128)S(1)} %get-tuple-element.122, ...), kind=kLoop, calls=%fused_computation.59 | loop fusion | flops 57647104 | bytes 12800000 | tf_op jit(solution)/shard_map/transpose(jvp(vmap()))/reduce_sum | solution.py:169
  176.9 23.4 %scatter_custom_fusion = f32[9,4096]{0,1:T(8,128)S(1)} fusion(s32[4096]{0:T(1024)} %bitcast.291, f32[4096,9]{1,0:T(8,128)} %copy.326, f32[]{:T(128)} %constant.91.clone.1), kind=kCustom, calls=%fused_computation.97 | custom fusion | flops 36864 | bytes 147968 | tf_op jit(solution)/shard_map/transpose(jvp(jit(_take)))/scatter-add | solution.py:201
  200.3 7.2 %fusion.129 = (f32[1,4096]{0,1:T(8,128)S(1)}, f32[1,4096]{0,1:T(8,128)}, f32[1,4096]{0,1:T(8,128)}, f32[1,4096]{0,1:T(8,128)}, f32[1,4096]{0,1:T(8,128)}, /*inde...) fusion(f32[9,4096]{0,1:T(8,128)S(1)} %scatter_custom_fusion), kind=kLoop, calls=%fused_computation.306 | loop fusion | bytes 294912 | tf_op jit(solution)/shard_map/transpose(jvp())/unstack | solution.py:144
  207.5 2.5 pad_add_fusion
  212.9 2.4 copy.358
  217.5 2.8 copy.360
  229.2 2.6 fusion.71
  240.9 31.4 %all_to_all.19 = f32[59,32,128]{2,0,1:T(8,128)S(1)} all-to-all(f32[59,32,128]{2,0,1:T(8,128)S(1)} %copy.334), channel_id=1, replica_groups=mesh['cell'=32,'view'=8] {'cell'}, dimensions={1} | all-to-all | bytes 1933312 | tf_op jit(solution)/shard_map/all_to_all | solution.py:209
  274.2 29.2 %scatter_custom_fusion.1 = f32[59,32768]{0,1:T(8,128)} fusion(s32[4096]{0:T(1024)} %bitcast.289, f32[4096,59]{1,0:T(8,128)S(1)} %copy.336, f32[]{:T(128)} %constant.91.clone.1), kind=kCustom, calls=%fused_computation.15 | custom fusion | flops 241664 | bytes 7733760 | tf_op jit(solution)/shard_map/scatter-add | solution.py:215
  304.1 94.0 %reduce-scatter.2.cloned.1.call-done = f32[59,4096]{0,1:T(8,128)} async-done(((f32[59,32768]{0,1:T(8,128)}), f32[59,4096]{0,1:T(8,128)}) %reduce-scatter.2.cloned.1.call-update) | async-done | bytes 966672 | tf_op jit(solution)/shard_map/reduce_scatter | solution.py:217
  398.0 3.2 copy.338
  (169 shorter events, 50.9 us)
Async XLA Ops:
  7.2 33.7 %all-to-all-start = ((s32[32,1,128]{2,1,0:T(1,128)}), s32[32,1,128]{2,1,0:T(1,128)S(1)}, u32[]{:S(2)}, u32[]{:S(2)}) async-start(s32[32,1,128]{2,1,0:T(1,128)} %bitcast.298), calls=%async_computation | async-start | bytes 32768 | tf_op jit(solution)/shard_map/all_to_all | solution.py:187
  58.1 12.3 %copy-start.22 = (s32[1,8,512]{2,1,0:T(8,128)S(1)}, s32[1,8,512]{2,1,0:T(8,128)}, u32[]{:S(2)}) copy-start(s32[1,8,512]{2,1,0:T(8,128)} %param.9) | copy-start | bytes 49156
  58.1 13.5 %copy-start.28 = (s32[8]{0:T(128)S(1)}, s32[8]{0:T(128)}, u32[]{:S(2)}) copy-start(s32[8]{0:T(128)} %param.10) | copy-start | bytes 100
  59.9 34.9 %all-to-all-start.1 = ((f32[59,32,128]{2,0,1:T(8,128)}), f32[59,32,128]{2,0,1:T(8,128)S(1)}, u32[]{:S(2)}, u32[]{:S(2)}) async-start(f32[59,32,128]{2,0,1:T(8,128)} %broadcast_select_fusion), calls=%async_computation.1 | async-start | bytes 2097152 | tf_op jit(solution)/shard_map/all_to_all | solution.py:192
  69.1 328.9 %reduce-scatter.2.cloned.1.call-start = ((), (), s32[]{:S(2)}) async-start(), calls=%async_computation.4 | async-start | bytes 18874368 | tf_op jit(solution)/shard_map/reduce_scatter | solution.py:217
  95.5 6.9 %copy-start.12 = (f32[1,32,128]{2,1,0:T(8,128)}, f32[1,32,128]{2,1,0:T(8,128)S(1)}, u32[]{:S(2)}) copy-start(f32[1,32,128]{2,1,0:T(8,128)S(1)} %get-tuple-element.94) | copy-start | bytes 49156
  95.6 6.9 %copy-start.13 = (f32[1,32,128]{2,1,0:T(8,128)}, f32[1,32,128]{2,1,0:T(8,128)S(1)}, u32[]{:S(2)}) copy-start(f32[1,32,128]{2,1,0:T(8,128)S(1)} %get-tuple-element.95) | copy-start | bytes 49156
  95.6 6.9 %copy-start.14 = (f32[1,32,128]{2,1,0:T(8,128)}, f32[1,32,128]{2,1,0:T(8,128)S(1)}, u32[]{:S(2)}) copy-start(f32[1,32,128]{2,1,0:T(8,128)S(1)} %get-tuple-element.96) | copy-start | bytes 49156
  96.3 6.2 %copy-start.10 = (f32[1,32,128]{2,1,0:T(8,128)}, f32[1,32,128]{2,1,0:T(8,128)S(1)}, u32[]{:S(2)}) copy-start(f32[1,32,128]{2,1,0:T(8,128)S(1)} %add_divide_fusion.2) | copy-start | bytes 49156
  103.5 17.8 %copy-start.27 = (pred[8,512]{1,0:T(8,128)(4,1)S(1)}, pred[8,512]{1,0:T(8,128)(4,1)}, u32[]{:S(2)}) copy-start(pred[8,512]{1,0:T(8,128)(4,1)} %compare_and_fusion.1) | copy-start | bytes 12292
  103.5 18.8 %copy-start.2 = (pred[8,4,128]{0,2,1:T(8,128)(4,1)S(1)}, pred[8,4,128]{0,2,1:T(8,128)(4,1)}, u32[]{:S(2)}) copy-start(pred[8,4,128]{0,2,1:T(8,128)(4,1)} %broadcast_compare_fusion) | copy-start | bytes 12292
  103.5 18.8 %copy-start.15 = (f32[8,256]{1,0:T(8,128)S(1)}, f32[8,256]{1,0:T(8,128)}, u32[]{:S(2)}) copy-start(f32[8,256]{1,0:T(8,128)} %convert_add_fusion) | copy-start | bytes 24580
  103.5 18.8 %copy-start.16 = (f32[8,256]{1,0:T(8,128)S(1)}, f32[8,256]{1,0:T(8,128)}, u32[]{:S(2)}) copy-start(f32[8,256]{1,0:T(8,128)} %convert_add_fusion.1) | copy-start | bytes 24580
  212.9 9.6 %copy-start.11 = (f32[1,32,128]{2,1,0:T(8,128)S(1)}, f32[1,32,128]{2,1,0:T(8,128)}, u32[]{:S(2)}) copy-start(f32[1,32,128]{2,1,0:T(8,128)} %copy-done.10) | copy-start | bytes 49156
  212.9 10.3 %copy-start = (f32[1,4096]{0,1:T(8,128)S(1)}, f32[1,4096]{0,1:T(8,128)}, u32[]{:S(2)}) copy-start(f32[1,4096]{0,1:T(8,128)} %get-tuple-element.72) | copy-start | bytes 49156
  215.2 8.6 %copy-start.4 = (f32[1,4096]{1,0:T(1,128)S(1)}, f32[1,4096]{1,0:T(1,128)}, u32[]{:S(2)}) copy-start(f32[1,4096]{1,0:T(1,128)} %copy-done.3) | copy-start | bytes 49156
  215.2 8.6 %copy-start.6 = (f32[1,4096]{1,0:T(1,128)S(1)}, f32[1,4096]{1,0:T(1,128)}, u32[]{:S(2)}) copy-start(f32[1,4096]{1,0:T(1,128)} %copy-done.5) | copy-start | bytes 49156
  223.1 16.6 %copy-start.7 = (f32[1,3,32,128]{3,2,1,0:T(8,128)S(1)}, f32[1,3,32,128]{3,2,1,0:T(8,128)}, u32[]{:S(2)}) copy-start(f32[1,3,32,128]{3,2,1,0:T(8,128)} %fusion.137) | copy-start | bytes 147460
  223.7 14.4 %copy-start.9 = (f32[32,128]{1,0:T(8,128)S(1)}, f32[32,128]{1,0:T(8,128)}, u32[]{:S(2)}) copy-start(f32[32,128]{1,0:T(8,128)} %copy-done.8) | copy-start | bytes 49156
  223.7 14.4 %copy-start.18 = (f32[1,32,128]{2,0,1:T(1,128)S(1)}, f32[1,32,128]{2,0,1:T(1,128)}, u32[]{:S(2)}) copy-start(f32[1,32,128]{2,0,1:T(1,128)} %get-tuple-element.78) | copy-start | bytes 49156
  223.7 14.4 %copy-start.19 = (f32[1,32,128]{2,0,1:T(1,128)S(1)}, f32[1,32,128]{2,0,1:T(1,128)}, u32[]{:S(2)}) copy-start(f32[1,32,128]{2,0,1:T(1,128)} %get-tuple-element.79) | copy-start | bytes 49156
  223.8 14.4 %copy-start.20 = (f32[1,32,128]{2,0,1:T(1,128)S(1)}, f32[1,32,128]{2,0,1:T(1,128)}, u32[]{:S(2)}) copy-start(f32[1,32,128]{2,0,1:T(1,128)} %get-tuple-element.80) | copy-start | bytes 49156
  223.8 14.4 %copy-start.21 = (f32[1,32,128]{2,0,1:T(1,128)S(1)}, f32[1,32,128]{2,0,1:T(1,128)}, u32[]{:S(2)}) copy-start(f32[1,32,128]{2,0,1:T(1,128)} %get-tuple-element.81) | copy-start | bytes 49156
  223.8 16.1 %copy-start.17 = (f32[1,4096]{1,0:T(1,128)S(1)}, f32[1,4096]{1,0:T(1,128)}, u32[]{:S(2)}) copy-start(f32[1,4096]{1,0:T(1,128)} %fusion.68) | copy-start | bytes 49156
  (8 other events, 15.9 us)
Sparse Core Ops, SparseCore 0:
  303.6 94.4 reduce-scatter.1
where the time goes:
time: 413 us; the launch traced here: 408 us
  other arithmetic  117 us (28%)
  waiting for transfers between devices  116 us (28%)
  local copies, waits for them, and re-layouts  87.4 us (21%)
  blocking collectives  31.4 us (8%)
  starting transfers between devices  21.8 us (5%)
  between operations  19.5 us (5%)
  matrix products  14.6 us (4%)
    reduce_scatter x1, waiting for transfers between devices, on_device(): lax.psum_scatter(summed, 'view', scatter_dimension=1, tiled=True)  94 us
    all_to_all x1, blocking collectives, on_device(): lax.all_to_all(grad_rows, 'cell', split_axis=1, concat_axis=1, tiled=True)  31.4 us
    unnamed x77, local copies, waits for them, and re-layouts  30.2 us
    scatter-add x1, other arithmetic, on_device(): summed = jnp.zeros(gaussians.shape, jnp.float32).at[:, held_flat].add(ret...  29.2 us
    scatter-add x1, other arithmetic, total_loss(): jnp.take(feature_table, picked, axis=1).reshape(9, tiles_dev, list_len)  23.4 us
    all_to_all x1, waiting for transfers between devices, on_device(): lax.all_to_all(payload, 'cell', split_axis=1, concat_axis=1, tiled=True)  22.4 us
    gather x2, local copies, waits for them, and re-layouts, total_loss(): jnp.take(feature_table, picked, axis=1).reshape(9, tiles_dev, list_len)  17.8 us
    gather x2, local copies, waits for them, and re-layouts, on_device(): columns = jnp.take(gaussians, flat_ids, axis=1)  17.2 us
  transfers between devices with their start and end apart: 3, of which 2 were waited for; matrix products, arithmetic and copies ran while one was open for 5% of the time, Pallas kernels for 0%

commit v1 on v0

v1 whole, which is shorter than its diff:
```python
import functools

import jax
import jax.numpy as jnp
import numpy as np
from jax import lax
from jax.experimental import pallas as pl
from jax.experimental.pallas import tpu as pltpu
from jax.sharding import PartitionSpec as P

MESH = pl.DeviceIdType.MESH
LOG2E = 1.4426950408889634
F32 = jnp.float32
BF16 = jnp.bfloat16

harmonic_zero = 0.28209479177387814
harmonic_one = 0.4886025119029199
harmonic_two = (
    1.0925484305920792,
    -1.0925484305920792,
    0.31539156525252005,
    -1.0925484305920792,
    0.5462742152960396,
)
harmonic_three = (
    -0.5900435899266435,
    2.890611442640554,
    -0.4570457994644658,
    0.3731763325901154,
    -0.4570457994644658,
    1.445305721320277,
    -0.5900435899266435,
)


def harmonic_basis(direction):
    along_x, along_y, along_z = (direction[0], direction[1], direction[2])
    square_x, square_y, square_z = (along_x * along_x, along_y * along_y, along_z * along_z)
    return [
        harmonic_zero + 0.0 * along_x,
        -harmonic_one * along_y,
        harmonic_one * along_z,
        -harmonic_one * along_x,
        harmonic_two[0] * along_x * along_y,
        harmonic_two[1] * along_y * along_z,
        harmonic_two[2] * (2.0 * square_z - square_x - square_y),
        harmonic_two[3] * along_x * along_z,
        harmonic_two[4] * (square_x - square_y),
        harmonic_three[0] * along_y * (3.0 * square_x - square_y),
        harmonic_three[1] * along_x * along_y * along_z,
        harmonic_three[2] * along_y * (4.0 * square_z - square_x - square_y),
        harmonic_three[3] * along_z * (2.0 * square_z - 3.0 * square_x - 3.0 * square_y),
        harmonic_three[4] * along_x * (4.0 * square_z - square_x - square_y),
        harmonic_three[5] * along_z * (square_x - square_y),
        harmonic_three[6] * along_x * (square_x - 3.0 * square_y),
    ]


def camera_columns(cams):
    cosine, sine = jnp.cos(cams), jnp.sin(cams)
    wide = lambda t, k: jnp.broadcast_to(t[:, k:k + 1], (8, 128))
    cos_yaw, cos_pitch, cos_roll = [wide(cosine, k) for k in range(3)]
    sin_yaw, sin_pitch, sin_roll = [wide(sine, k) for k in range(3)]
    shift_u, shift_v, scale_u, scale_v = [wide(cams, k) for k in range(3, 7)]
    first = [
        cos_yaw * cos_pitch,
        cos_yaw * sin_pitch * sin_roll - sin_yaw * cos_roll,
        cos_yaw * sin_pitch * cos_roll + sin_yaw * sin_roll,
    ]
    second = [
        sin_yaw * cos_pitch,
        sin_yaw * sin_pitch * sin_roll + cos_yaw * cos_roll,
        sin_yaw * sin_pitch * cos_roll - cos_yaw * sin_roll,
    ]
    third = [-sin_pitch, cos_pitch * sin_roll, cos_pitch * cos_roll]
    return (
        [scale_u * t for t in first] + [64.0 + shift_u]
        + [scale_v * t for t in second] + [256.0 + shift_v]
        + harmonic_basis(third)
    )


def place():
    cell, view = lax.axis_index("cell"), lax.axis_index("view")
    return cell, view, cell >> 2, cell & 3, view >> 1, view & 1


def requester(i, z, y, x, core):
    dz = core + 2 * i
    return (((z + dz) & 7) << 2) | ((y + x - dz) & 3)


def server(i, z, y, x, core):
    dz = core + 2 * i
    return (((z - dz) & 7) << 2) | ((y - x + dz) & 3)


def greet():
    cell, view, z, y, x, core = place()
    barrier = pltpu.get_barrier_semaphore()

    def signal(where, who):
        pl.semaphore_signal(barrier, inc=1, device_id=(where, who), device_id_type=MESH)

    for i in range(4):
        if i == 0:
            @pl.when(view != 0)
            def _():
                signal(requester(0, z, y, x, core), view)
                signal(server(0, z, y, x, core), view)
        else:
            signal(requester(i, z, y, x, core), view)
            signal(server(i, z, y, x, core), view)
    for step in range(1, 8):
        signal(cell, (view + step) & 7)
    pl.semaphore_wait(barrier, jnp.where(view == 0, 13, 15))


class Or_local:
    def __init__(self, i, view, remote, local):
        self.first, self.view, self.remote, self.local = i == 0, view, remote, local

    def each(self, remote_act, local_act):
        if not self.first:
            remote_act(self.remote())
            return

        if local_act is not None:
            @pl.when(self.view == 0)
            def _():
                local_act(self.local())

        @pl.when(self.view != 0)
        def _():
            remote_act(self.remote())

    def start(self):
        self.each(lambda c: c.start(), lambda c: c.start())

    def wait_recv(self):
        self.each(lambda c: c.wait_recv(), lambda c: c.wait())

    def wait_send(self):
        self.each(lambda c: c.wait_send(), None)


def remote(source, target, send, recv, where, who):
    return pltpu.make_async_remote_copy(
        src_ref=source, dst_ref=target, send_sem=send, recv_sem=recv,
        device_id=(where, who), device_id_type=MESH,
    )


def rotation_of(values):
    scales = [jnp.exp(values[3 + k]) for k in range(3)]
    norm = jnp.sqrt(
        values[6] * values[6] + values[7] * values[7] + values[8] * values[8] + values[9] * values[9]
    )
    inverse = 1.0 / jnp.maximum(norm, 0.5)
    qw, qx, qy, qz = [values[6 + k] * inverse for k in range(4)]
    turned = [
        [1.0 - 2.0 * (qy * qy + qz * qz), 2.0 * (qx * qy - qw * qz), 2.0 * (qx * qz + qw * qy)],
        [2.0 * (qx * qy + qw * qz), 1.0 - 2.0 * (qx * qx + qz * qz), 2.0 * (qy * qz - qw * qx)],
        [2.0 * (qx * qz - qw * qy), 2.0 * (qy * qz + qw * qx), 1.0 - 2.0 * (qx * qx + qy * qy)],
    ]
    return scales, (qw, qx, qy, qz), norm, inverse, turned


def conic_of(consts, scaled):
    first = [sum(consts[r] * scaled[r][k] for r in range(3)) for k in range(3)]
    second = [sum(consts[4 + r] * scaled[r][k] for r in range(3)) for k in range(3)]
    uu = first[0] * first[0] + first[1] * first[1] + first[2] * first[2] + 0.3
    uv = first[0] * second[0] + first[1] * second[1] + first[2] * second[2]
    vv = second[0] * second[0] + second[1] * second[1] + second[2] * second[2] + 0.3
    det = uu * vv - uv * uv
    return vv / det, -uv / det, uu / det


def log_sigmoid(x):
    return jnp.minimum(x, 0.0) - jnp.log(1.0 + jnp.exp(-jnp.abs(x)))


def ask_kernel(
    cam_ref, fetch_ref, ids_out, cams_out,
    row, cams, idv, loc_sem, id_send, id_recv, cam_send, cam_recv,
):
    cell, view, z, y, x, core = place()
    row[...] = jnp.zeros_like(row)
    row[:, 0:7] = cam_ref[...]
    greet()

    def id_copy(i):
        owner = server(i, z, y, x, core)
        source, target = fetch_ref.at[pl.ds(owner, 1)], idv.at[pl.ds(i, 1)]
        return Or_local(
            i, view,
            lambda: remote(source, target, id_send.at[i], id_recv.at[i], owner, view),
            lambda: pltpu.make_async_copy(source, target, id_recv.at[i]),
        )

    def cam_copy(step):
        return remote(
            row, cams.at[pl.ds(view, 1)], cam_send.at[step], cam_recv.at[step],
            cell, (view + step) & 7,
        )

    for i in range(4):
        id_copy(i).start()
    for step in range(1, 8):
        cam_copy(step).start()
    mine = pltpu.make_async_copy(row, cams.at[pl.ds(view, 1)], loc_sem)
    mine.start()
    for i in range(4):
        id_copy(i).wait_recv()
    ids_out[...] = idv[...]
    for step in range(1, 8):
        cam_copy(step).wait_recv()
    mine.wait()
    cams_out[...] = cams[...]
    for i in range(4):
        id_copy(i).wait_send()
    for step in range(1, 8):
        cam_copy(step).wait_send()


def project_kernel(
    ids_ref, cams_ref, gauss_ref, feat_out, params_out, consts_out, tab, got, sem,
):
    cell, view, z, y, x, core = place()
    whole = pltpu.make_async_copy(gauss_ref, tab, sem)
    whole.start()
    consts = camera_columns(cams_ref[...])
    lanes = lax.broadcasted_iota(jnp.int32, (8, 128), 1)
    packed = jnp.zeros((8, 128), F32)
    for k in range(24):
        packed = jnp.where(lanes == k, consts[k], packed)
    consts_out[...] = packed
    lane = lax.broadcasted_iota(jnp.int32, (59, 128), 1)
    whole.wait()

    def serve(i, carry):
        acc = jnp.zeros((59, 128), F32)
        for n in range(128):
            name = ids_ref[i, n]
            block = tab[:, pl.ds(pl.multiple_of((name >> 7) << 7, 128), 128)]
            acc = jnp.where(lane == n, pltpu.roll(block, (n - name) & 127, 1), acc)
        got[0:59] = acc
        params_out[i] = got[0:16]
        values = [got[k:k + 1] for k in range(59)]
        served = requester(i, z, y, x, core)
        screen_u = sum(consts[r] * values[r] for r in range(3)) + consts[3]
        screen_v = sum(consts[4 + r] * values[r] for r in range(3)) + (
            consts[7] - (16 * served + 8).astype(F32)
        )
        scales, _q, _norm, _inverse, turned = rotation_of(values)
        scaled = [[turned[r][k] * scales[k] for k in range(3)] for r in range(3)]
        conic_a, conic_b, conic_c = conic_of(consts, scaled)
        colours = [
            0.5 + sum(consts[8 + k] * values[11 + 3 * k + c] for k in range(16)) for c in range(3)
        ]
        log_opacity = jnp.broadcast_to(log_sigmoid(values[10]), (8, 128))
        rows = [screen_u, screen_v, conic_a, conic_b, conic_c, log_opacity] + colours
        for f in range(9):
            feat_out[i, f] = rows[f]
        return carry

    lax.fori_loop(0, 4, serve, 0)


def three(x):
    high = x.astype(BF16).astype(F32)
    rest = x - high
    middle = rest.astype(BF16).astype(F32)
    return high, middle, rest - middle


def dot_nn(a, b):
    return lax.dot_general(a, b, (((1,), (0,)), ((), ())), preferred_element_type=F32)


def dot_nt(a, b):
    return lax.dot_general(a, b, (((1,), (1,)), ((), ())), preferred_element_type=F32)


def dot_tn(a, b):
    return lax.dot_general(a, b, (((0,), (0,)), ((), ())), preferred_element_type=F32)


CHUNK = 512


def composite(
    table_ref, list_ref, target_ref, basis_ref, basis_t_ref, rendered_out,
    onehot, feats, alpha, weight, weight_h, weight_m, colour_rows, image, grad_chunk, slot_acc,
):
    steps = CHUNK // 8
    chunks = 4096 // CHUNK
    table = table_ref[...].reshape(144, 256)
    table3 = jnp.concatenate(three(table), axis=0).astype(BF16)
    tile_of = lax.broadcasted_iota(jnp.int32, (1, CHUNK), 1) & 7
    in_tile = lax.broadcasted_iota(jnp.int32, (8, CHUNK), 0) == tile_of
    low_iota = lax.broadcasted_iota(jnp.int32, (256, CHUNK), 0)
    high_iota = lax.broadcasted_iota(jnp.int32, (16, CHUNK), 0)
    zeros_row = jnp.zeros((1, CHUNK), F32)
    image[...] = jnp.zeros_like(image)
    slot_acc[...] = jnp.zeros_like(slot_acc)

    def forward(k, through):
        cols = pl.ds(pl.multiple_of(k * CHUNK, CHUNK), CHUNK)
        index = list_ref[:, cols]
        hot = jnp.where(low_iota == (index & 255), 1.0, 0.0).astype(BF16)
        onehot[:, cols] = hot
        picked = dot_nn(table3, hot)
        picked = picked[0:144] + picked[144:288] + picked[288:432]
        here = high_iota == (index >> 8)
        rows = [
            jnp.sum(jnp.where(here, picked[f * 16:(f + 1) * 16], 0.0), axis=0, keepdims=True)
            for f in range(9)
        ]
        u = rows[0] - (16 * tile_of + 8).astype(F32)
        v, a, b, c, log_opacity = rows[1:6]
        feats[0:1, cols] = u
        feats[1:2, cols] = v
        feats[2:3, cols] = a
        feats[3:4, cols] = b
        feats[4:5, cols] = c
        live = index >= 0
        along_u = a * u + b * v
        along_v = b * u + c * v
        constant = jnp.where(live, log_opacity - 0.5 * (along_u * u + along_v * v), -16384.0)
        terms = [constant, along_u, along_v, -0.5 * a, -b, -0.5 * c]
        terms = [t * LOG2E for t in terms] + [zeros_row, zeros_row]
        terms = jnp.concatenate(terms, axis=0)
        high, middle, low = three(terms)
        terms = jnp.concatenate([high, middle, low, jnp.zeros_like(low)], axis=0).astype(BF16)
        power = dot_tn(terms, basis_ref[...])
        seen = jnp.minimum(jnp.exp2(power), 0.99)
        alpha[cols, :] = seen
        for j in range(steps):
            one = seen[8 * j:8 * j + 8]
            part = through * one
            weight[pl.ds(pl.multiple_of(k * CHUNK + 8 * j, 8), 8), :] = part
            through = through - part
        part = weight[cols, :]
        part_h = part.astype(BF16)
        part_m = (part - part_h.astype(F32)).astype(BF16)
        weight_h[cols, :] = part_h
        weight_m[cols, :] = part_m
        masked = jnp.concatenate(
            [jnp.where(in_tile, rows[6 + ch], 0.0) for ch in range(3)], axis=0
        )
        high, middle, low = three(masked)
        stacked = jnp.concatenate([high, middle, low, high, middle, high], axis=0).astype(BF16)
        colour_rows[:, cols] = stacked
        image[...] += dot_nn(stacked[0:80], part_h) + dot_nn(stacked[0:80], part_m)
        return through

    lax.fori_loop(0, chunks, forward, jnp.ones((8, 256), F32))
    picture = image[0:24] + image[24:48] + image[48:72]
    rendered_out[...] = picture
    wrong = picture - target_ref[...]
    high, middle, low = three(wrong)
    wrong_q = jnp.concatenate([high, high, high, middle, middle, low], axis=0).astype(BF16)
    wrong_w = jnp.concatenate([high, middle], axis=0).astype(BF16)

    def backward(step, behind):
        k = chunks - 1 - step
        cols = pl.ds(pl.multiple_of(k * CHUNK, CHUNK), CHUNK)
        value = dot_tn(colour_rows[:, cols], wrong_q)
        for j in reversed(range(steps)):
            at = pl.ds(pl.multiple_of(k * CHUNK + 8 * j, 8), 8)
            seen = alpha[at, :]
            gain = value[8 * j:8 * j + 8] - behind
            grad_chunk[8 * j:8 * j + 8, :] = jnp.where(seen < 0.99, weight[at, :] * gain, 0.0)
            behind = behind + seen * gain
        grad = grad_chunk[...]
        high, middle, low = three(grad)
        basis_t = basis_t_ref[...]
        moments = (
            dot_nt(basis_t, high.astype(BF16))
            + dot_nt(basis_t, middle.astype(BF16))
            + dot_nt(basis_t, low.astype(BF16))
        )
        tinted = dot_nt(wrong_w, weight_h[cols, :]) + dot_nt(wrong_w, weight_m[cols, :])
        tinted = tinted[0:24] + tinted[24:48]
        colour = [
            jnp.sum(jnp.where(in_tile, tinted[8 * ch:8 * ch + 8], 0.0), axis=0, keepdims=True)
            for ch in range(3)
        ]
        u, v, a, b, c = [feats[f:f + 1, cols] for f in range(5)]
        m1, mx, my, mxx, mxy, myy = [moments[f:f + 1] for f in range(6)]
        dx = mx - u * m1
        dy = my - v * m1
        found = [
            a * dx + b * dy,
            b * dx + c * dy,
            -0.5 * (mxx - u * (mx + dx)),
            -(mxy - u * my - v * dx),
            -0.5 * (myy - v * (my + dy)),
            m1,
        ] + colour
        found = jnp.concatenate(found + [zeros_row] * 7, axis=0)
        index = list_ref[:, cols]
        here = high_iota == (index >> 8)
        spread = [
            jnp.where(here, part[f:f + 1], 0.0) for part in three(found) for f in range(9)
        ]
        spread = jnp.concatenate(spread, axis=0).astype(BF16)
        slot_acc[...] += dot_nt(spread, onehot[:, cols])
        return behind

    lax.fori_loop(0, chunks, backward, jnp.zeros((8, 256), F32))
    total = slot_acc[0:144] + slot_acc[144:288] + slot_acc[288:432]
    return total


def window_kernel(
    feat_ref, params_ref, consts_ref, ids_ref, list_ref, target_ref, basis_ref, basis_t_ref,
    rendered_out, all_out,
    came, by_server, table, onehot, feats, alpha, weight, weight_h, weight_m, colour_rows, image,
    grad_chunk, slot_acc, to_server, back, got, gathered,
    out_send, out_recv, in_send, in_recv, back_send, back_recv, own_send, own_recv,
    far_send, far_recv, near_send, near_recv, loc_sem,
):
    cell, view, z, y, x, core = place()
    greet()

    def feature_out(i):
        source, target = feat_ref.at[i], came.at[i]
        return Or_local(
            i, view,
            lambda: remote(
                source, target, out_send.at[i], out_recv.at[i],
                requester(i, z, y, x, core), view,
            ),
            lambda: pltpu.make_async_copy(source, target, out_recv.at[i]),
        )

    def feature_in(step):
        who = (view + step) & 7
        return remote(
            came.at[:, :, who, :], by_server.at[view], in_send.at[step], in_recv.at[step], cell, who
        )

    for i in range(4):
        feature_out(i).start()
    for i in range(4):
        feature_out(i).wait_recv()
    for step in range(1, 8):
        feature_in(step).start()
    mine = pltpu.make_async_copy(came.at[:, :, view, :], by_server.at[view], loc_sem.at[0])
    mine.start()
    for i in range(4):
        feature_out(i).wait_send()
    mine.wait()
    for step in range(1, 8):
        feature_in(step).wait_recv()
    for step in range(1, 8):
        feature_in(step).wait_send()
    for who in range(8):
        for i in range(4):
            row, lanes = 2 * who + i // 2, slice((i % 2) * 128, (i % 2) * 128 + 128)
            for f in range(9):
                table[f, row:row + 1, lanes] = by_server[who, i, f:f + 1]

    total = composite(
        table, list_ref, target_ref, basis_ref, basis_t_ref, rendered_out,
        onehot, feats, alpha, weight, weight_h, weight_m, colour_rows, image, grad_chunk, slot_acc,
    )

    slot_acc[0:144] = total
    for who in range(8):
        for i in range(4):
            row, lanes = 2 * who + i // 2, slice((i % 2) * 128, (i % 2) * 128 + 128)
            for f in range(9):
                to_server[who, i, f:f + 1] = slot_acc[16 * f + row:16 * f + row + 1, lanes]

    def grad_back(step):
        who = (view + step) & 7
        return remote(
            to_server.at[who], back.at[:, :, view, :], back_send.at[step], back_recv.at[step],
            cell, who,
        )

    def grad_own(i):
        source, target = back.at[i], got.at[i]
        return Or_local(
            i, view,
            lambda: remote(
                source, target, own_send.at[i], own_recv.at[i], server(i, z, y, x, core), view
            ),
            lambda: pltpu.make_async_copy(source, target, own_recv.at[i]),
        )

    for step in range(1, 8):
        grad_back(step).start()
    mine = pltpu.make_async_copy(to_server.at[view], back.at[:, :, view, :], loc_sem.at[1])
    mine.start()
    mine.wait()
    for step in range(1, 8):
        grad_back(step).wait_recv()
    for i in range(4):
        grad_own(i).start()
    consts = [jnp.broadcast_to(consts_ref[:, k:k + 1], (8, 128)) for k in range(8)]
    for i in range(4):
        grad_own(i).wait_recv()
        values = [params_ref[i, k:k + 1] for k in range(11)]
        scales, (qw, qx, qy, qz), norm, inverse, turned = rotation_of(values)
        scaled = [[turned[r][k] * scales[k] for k in range(3)] for r in range(3)]
        a, b, c = conic_of(consts, scaled)
        du, dv, da, db, dc, dlog, d0, d1, d2 = [got[i, f] for f in range(9)]
        down = lambda t: jnp.sum(t, axis=0, keepdims=True)
        position = [down(consts[r] * du + consts[4 + r] * dv) for r in range(3)]
        half = 0.5 * db
        p00 = a * da + b * half
        p01 = a * half + b * dc
        p10 = b * da + c * half
        p11 = b * half + c * dc
        s00 = -(p00 * a + p01 * b)
        s01 = -(p00 * b + p01 * c)
        s11 = -(p10 * b + p11 * c)
        cov = {}
        for r in range(3):
            first = consts[r] * s00 + consts[4 + r] * s01
            second = consts[r] * s01 + consts[4 + r] * s11
            for t in range(r, 3):
                cov[r, t] = down(first * consts[t] + second * consts[4 + t])
                cov[t, r] = cov[r, t]
        dscaled = [
            [2.0 * sum(cov[r, t] * scaled[t][k] for t in range(3)) for k in range(3)]
            for r in range(3)
        ]
        dlogs = [sum(dscaled[r][k] * scaled[r][k] for r in range(3)) for k in range(3)]
        (e00, e01, e02), (e10, e11, e12), (e20, e21, e22) = [
            [dscaled[r][k] * scales[k] for k in range(3)] for r in range(3)
        ]
        qd = [
            2.0 * (qz * (e10 - e01) + qy * (e02 - e20) + qx * (e21 - e12)),
            2.0 * (qy * (e01 + e10) + qz * (e02 + e20) + qw * (e21 - e12) - 2.0 * qx * (e11 + e22)),
            2.0 * (qx * (e01 + e10) + qw * (e02 - e20) + qz * (e12 + e21) - 2.0 * qy * (e00 + e22)),
            2.0 * (qw * (e10 - e01) + qx * (e02 + e20) + qy * (e12 + e21) - 2.0 * qz * (e00 + e11)),
        ]
        inward = jnp.where(norm > 0.5, qw * qd[0] + qx * qd[1] + qy * qd[2] + qz * qd[3], 0.0)
        dq = [(g - q * inward) * inverse for g, q in zip(qd, (qw, qx, qy, qz))]
        dlogit = down(dlog) * (1.0 / (1.0 + jnp.exp(values[10])))
        name = ids_ref[i:i + 1].astype(F32)
        zero = jnp.zeros_like(name)
        rows = position + dlogs + dq + [dlogit, name] + [zero] * 4
        cols = pl.ds(i * 128, 128)
        gathered[view, 0:16, cols] = jnp.concatenate(rows, axis=0)
        gathered[view, 16:24, cols] = d0
        gathered[view, 24:32, cols] = d1
        gathered[view, 32:40, cols] = d2


    def far(step):
        who = (view + 2 * step) & 7
        return remote(
            gathered.at[view], gathered.at[view], far_send.at[step], far_recv.at[step], cell, who
        )

    def near(step):
        which = (view - 2 * step) & 7
        return remote(
            gathered.at[which], gathered.at[which], near_send.at[step], near_recv.at[step],
            cell, view ^ 1,
        )

    for step in (2, 1, 3):
        far(step).start()
    near(0).start()
    for step in (1, 3, 2):
        which = (view - 2 * step) & 7
        pltpu.make_async_copy(gathered.at[view], gathered.at[which], far_recv.at[step]).wait()
        near(step).start()
    for step in range(4):
        which = ((view ^ 1) - 2 * step) & 7
        pltpu.make_async_copy(gathered.at[view], gathered.at[which], near_recv.at[step]).wait()
    for step in range(1, 8):
        grad_back(step).wait_send()
    for i in range(4):
        grad_own(i).wait_send()
    for step in (1, 2, 3):
        far(step).wait_send()
    for step in range(4):
        near(step).wait_send()
    all_out[...] = gathered[...]


def place_kernel(base_ref, all_ref, mix_ref, out_ref, acc):
    base = base_ref[0]
    low_iota = lax.broadcasted_iota(jnp.int32, (256, 512), 0)
    acc[...] = jnp.zeros_like(acc)

    def one(source, carry):
        block = all_ref[source]
        name = block[11:12].astype(jnp.int32) - base
        hot = jnp.where(low_iota == (name & 255), 1.0, 0.0).astype(BF16)
        high = name >> 8
        parts = jnp.concatenate(three(block), axis=0)
        spread = jnp.concatenate(
            [
                jnp.concatenate(
                    [jnp.where(high == h, parts, 0.0), jnp.where(high == h + 1, parts, 0.0)], axis=0
                ).astype(BF16)
                for h in range(0, 16, 2)
            ],
            axis=0,
        )
        acc[...] += dot_nt(spread, hot)
        return carry

    lax.fori_loop(0, 8, one, 0)
    mix = mix_ref[...]
    for h in range(16):
        at = 120 * h
        found = acc[at:at + 40] + acc[at + 40:at + 80] + acc[at + 80:at + 120]
        out_ref[:, h * 256:(h + 1) * 256] = jnp.dot(
            mix, found, precision=lax.Precision.HIGHEST, preferred_element_type=F32
        )


def pixel_basis():
    pixel = np.arange(256)
    x = pixel % 16 - 7.5
    y = pixel // 16 - 7.5
    eight = np.stack([np.ones(256), x, y, x * x, x * y, y * y, 0 * x, 0 * x])
    wide = np.concatenate([eight, eight, eight, 0 * eight]).astype(np.float32)
    tall = np.concatenate([eight, 0 * eight]).astype(np.float32)
    return jnp.asarray(wide, BF16), jnp.asarray(tall, BF16)


VM = pl.BlockSpec(memory_space=pltpu.VMEM)
SM = pl.BlockSpec(memory_space=pltpu.SMEM)
MIB = 1024 * 1024
DMA = pltpu.SemaphoreType.DMA


def shape(*dims, dtype=F32):
    return jax.ShapeDtypeStruct(dims, dtype)


def ask(camera, ids):
    return pl.pallas_call(
        ask_kernel,
        out_shape=(shape(4, 128, dtype=jnp.int32), shape(8, 128)),
        in_specs=[VM, VM],
        out_specs=(VM, VM),
        scratch_shapes=[
            pltpu.VMEM((1, 128), F32),
            pltpu.VMEM((8, 128), F32),
            pltpu.VMEM((4, 128), jnp.int32),
            DMA, DMA((4,)), DMA((4,)), DMA((8,)), DMA((8,)),
        ],
        compiler_params=pltpu.CompilerParams(
            collective_id=0, has_side_effects=True, vmem_limit_bytes=2 * MIB
        ),
        name="ask",
    )(camera, ids)


def project(ids, cams, gaussians):
    return pl.pallas_call(
        project_kernel,
        out_shape=(shape(4, 9, 8, 128), shape(4, 16, 128), shape(8, 128)),
        in_specs=[SM, VM, pl.BlockSpec(memory_space=pl.ANY)],
        out_specs=(VM, VM, VM),
        scratch_shapes=[pltpu.VMEM((59, 32768), F32), pltpu.VMEM((64, 128), F32), DMA],
        compiler_params=pltpu.CompilerParams(vmem_limit_bytes=16 * MIB),
        name="project",
    )(ids, cams, gaussians)


def window(feat, params, consts, ids, listed, target):
    wide, tall = pixel_basis()
    return pl.pallas_call(
        window_kernel,
        out_shape=(shape(24, 256), shape(8, 40, 512)),
        in_specs=[VM] * 8,
        out_specs=(VM, VM),
        scratch_shapes=[
            pltpu.VMEM((4, 9, 8, 128), F32),
            pltpu.VMEM((8, 4, 9, 128), F32),
            pltpu.VMEM((9, 16, 256), F32),
            pltpu.VMEM((256, 4096), BF16),
            pltpu.VMEM((8, 4096), F32),
            pltpu.VMEM((4096, 256), F32),
            pltpu.VMEM((4096, 256), F32),
            pltpu.VMEM((4096, 256), BF16),
            pltpu.VMEM((4096, 256), BF16),
            pltpu.VMEM((144, 4096), BF16),
            pltpu.VMEM((80, 256), F32),
            pltpu.VMEM((CHUNK, 256), F32),
            pltpu.VMEM((432, 256), F32),
            pltpu.VMEM((8, 4, 9, 128), F32),
            pltpu.VMEM((4, 9, 8, 128), F32),
            pltpu.VMEM((4, 9, 8, 128), F32),
            pltpu.VMEM((8, 40, 512), F32),
            DMA((4,)), DMA((4,)), DMA((8,)), DMA((8,)), DMA((8,)), DMA((8,)), DMA((4,)), DMA((4,)),
            DMA((4,)), DMA((4,)), DMA((4,)), DMA((4,)), DMA((2,)),
        ],
        compiler_params=pltpu.CompilerParams(
            collective_id=1, has_side_effects=True, vmem_limit_bytes=48 * MIB
        ),
        name="window",
    )(feat, params, consts, ids, listed, target, wide, tall)


def put(base, everything, mix):
    return pl.pallas_call(
        place_kernel,
        out_shape=shape(59, 4096),
        in_specs=[SM, VM, VM],
        out_specs=VM,
        scratch_shapes=[pltpu.VMEM((1920, 256), F32)],
        compiler_params=pltpu.CompilerParams(vmem_limit_bytes=32 * MIB),
        name="put",
    )(base, everything, mix)


def mixing(consts):
    harmonics = consts[:, 8:24].T
    spread = harmonics[:, None, None, :] * jnp.eye(3, dtype=F32)[None, :, :, None]
    colour = jnp.pad(spread.reshape(48, 24), ((11, 0), (16, 0)))
    return colour + jnp.asarray(np.eye(59, 40) * (np.arange(59) < 11)[:, None], F32)


def slots_of(entries):
    _cell, _view, z, y, _x, _core = place()
    owner = entries >> 7
    dz = (z - (owner >> 2)) & 7
    dy = (y - (owner & 3)) & 3
    who = (((dy + dz) & 3) << 1) | (dz & 1)
    return (((who << 2) | (dz >> 1)) << 7) | (entries & 127)


def on_device(gaussians, cameras, fetch_ids, tile_lists, lengths, target_image):
    live = jnp.arange(512, dtype=jnp.int32)[:, None] < lengths[None, :]
    listed = jnp.where(live, slots_of(tile_lists[0]).T, -1).reshape(1, 4096)
    target = target_image.reshape(24, 256)
    ids, cams = ask(cameras, fetch_ids[0])
    feat, params, consts = project(ids, cams, gaussians)
    picture, everything = window(feat, params, consts, ids, listed, target)
    base = (lax.axis_index("view") * 4096).astype(jnp.int32).reshape(1)
    param_grads = put(base, everything, mixing(consts))
    return picture.reshape(3, 1, 8, 256), param_grads


def solution(mesh):
    in_specs = (
        P(None, "cell"),
        P("view", None),
        P("cell", None, None),
        P("view", "cell", None),
        P("cell"),
        P(None, "view", "cell", None),
    )
    out_specs = (P(None, "view", "cell", None), P(None, ("cell", "view")))
    return jax.shard_map(
        on_device, mesh=mesh, in_specs=in_specs, out_specs=out_specs, check_vma=False
    )
```

time: 413 us -> 91 us (0.22); the launches traced: 408 us -> 90.7 us
  other arithmetic: 117 us -> 0.96 us
  waiting for transfers between devices: 116 us -> 0 us
  Pallas kernels: 0 us -> 83.1 us
  local copies, waits for them, and re-layouts: 87.4 us -> 5.91 us
  blocking collectives: 31.4 us -> 0 us
  starting transfers between devices: 21.8 us -> 0 us
  between operations: 19.5 us -> 0.74 us
  matrix products: 14.6 us -> 0 us
    reduce_scatter x1 -> x0, waiting for transfers between devices: 94 us -> none  [on_device(): lax.psum_scatter(summed, 'view', scatter_dimension=1, tiled=True)]
    pallas_call x0 -> x4, Pallas kernels: none -> 83.1 us  [the longest x1 53.8 us: window(): pl.pallas_call(window_kernel, out_shape=(shape(24, 256), shape(8, 40, 512...]
    scatter-add x2 -> x0, other arithmetic: 52.6 us -> none  [the longest x1 29.2 us: on_device(): summed = jnp.zeros(gaussians.shape, jnp.float32).at[:, held_flat].add(ret...]
    gather x4 -> x0, local copies, waits for them, and re-layouts: 34.9 us -> none  [the longest x2 17.8 us: total_loss(): jnp.take(feature_table, picked, axis=1).reshape(9, tiles_dev, list_len)]
    all_to_all x1 -> x0, blocking collectives: 31.4 us -> none  [on_device(): lax.all_to_all(grad_rows, 'cell', split_axis=1, concat_axis=1, tiled=True)]
    unnamed x77 -> x15, local copies, waits for them, and re-layouts: 30.2 us -> 5.37 us
    all_to_all x2 -> x0, waiting for transfers between devices: 22.4 us -> none  [the longest x1 22.4 us: on_device(): lax.all_to_all(payload, 'cell', split_axis=1, concat_axis=1, tiled=True)]
    all_to_all x2 -> x0, starting transfers between devices: 21.3 us -> none  [the longest x1 12 us: on_device(): lax.all_to_all(requests, 'cell', split_axis=0, concat_axis=0, tiled=True)]
  transfers between devices with their start and end apart: 3 -> 0, of which waited for: 2 -> 0; matrix products, arithmetic and copies ran while one was open for 5% -> 0% of each run, Pallas kernels for 0% -> 0%
where the time goes in v1:
time: 91 us; the launch traced here: 90.7 us
  Pallas kernels  83.1 us (91%)
  local copies, waits for them, and re-layouts  5.91 us (6%)
  other arithmetic  0.96 us (1%)
    pallas_call x1, Pallas kernels, window(): pl.pallas_call(window_kernel, out_shape=(shape(24, 256), shape(8, 40, 512...  53.8 us
    pallas_call x1, Pallas kernels, ask(): pl.pallas_call(ask_kernel, out_shape=(shape(4, 128, dtype=jnp.int32), sha...  15.5 us
    pallas_call x1, Pallas kernels, put(): pl.pallas_call(place_kernel, out_shape=shape(59, 4096), in_specs=[SM, VM,...  7.79 us
    pallas_call x1, Pallas kernels, project(): pl.pallas_call(project_kernel, out_shape=(shape(4, 9, 8, 128), shape(4, 1...  6.05 us
    unnamed x15, local copies, waits for them, and re-layouts  5.37 us

profile of v1, /device:TPU:1, one launch (start us, length us, event | category | flops | bytes accessed | tf_op | source)
XLA Modules:
  0.0 90.7 jit_solution(18047474042781438214)
XLA Ops:
  0.6 0.0 copy-start.1
  0.7 0.0 copy-start.2
  0.7 0.7 copy-done.2
  1.4 0.0 copy-start.5
  1.4 0.7 copy-done.5
  2.0 0.0 copy-start.3
  2.0 15.5 %ask.1 = (s32[4,128]{1,0:T(4,128)S(1)}, f32[8,128]{1,0:T(8,128)S(1)}) custom-call(f32[1,7]{1,0:T(1,128)S(1)} %copy-done.5, s32[32,128]{1,0:T(8,128)S(1)} %bitcast.14), custom_call_target="tpu_custom_call" | custom-call | tf_op jit(solution)/shard_map/ask/pallas_call | solution.py:644
  17.5 0.8 bitcast_select_fusion
  18.3 3.4 %copy-done = f32[59,32768]{1,0:T(8,128)S(1)} copy-done((f32[59,32768]{1,0:T(8,128)S(1)}, f32[59,32768]{1,0:T(8,128)}, u32[]{:S(2)}) %copy-start) | copy-done | bytes 7733272
  21.7 6.1 %project.1 = (f32[4,9,8,128]{3,2,1,0:T(8,128)S(1)}, f32[4,16,128]{2,1,0:T(8,128)S(1)}, f32[8,128]{1,0:T(8,128)S(1)}) custom-call(s32[4,128]{1,0:T(4,128)S(1)} %get-tuple-element.9.ids_ref, f32[8,128]{1,0:T(8,128)S(1)} %get-tuple-element.10.cams_ref, f32[59,32768]{1,0:T(8,128)S(1)} %copy-done), custom_call_target="tpu_custom_call" | custom-call | tf_op jit(solution)/shard_map/project/pallas_call | solution.py:663
  27.8 0.1 slice_bitcast_fusion
  27.8 0.1 copy.15
  27.9 0.1 broadcast_multiply_fusion
  28.0 0.1 mul.24
  28.1 0.0 copy-done.6
  28.1 0.1 pad_add_fusion.mix_ref
  28.2 0.1 copy.14
  28.3 0.2 reshape.46.list_ref
  28.5 0.0 copy-done.1
  28.5 0.0 copy-done.3
  28.5 0.0 copy-done.4
  28.5 53.8 %window.1 = (f32[24,256]{1,0:T(8,128)S(1)}, f32[8,40,512]{2,1,0:T(8,128)S(1)}) custom-call(f32[4,9,8,128]{3,2,1,0:T(8,128)S(1)} %get-tuple-element.11.feat_ref, f32[4,16,128]{2,1,0:T(8,128)S(1)} %get-tuple-element.12.params_ref, f32[8,128]{1,0:T(8,128)S(1)} %get-tuple-element.13.consts_ref, s32[4,128]{1,0:T(4,128)S(1)} %get-tuple-element.9.ids_ref, ...), custom_call_target="tpu_custom_call" | custom-call | tf_op jit(solution)/shard_map/window/pallas_call | solution.py:676
  82.3 7.8 %put.1 = f32[59,4096]{1,0:T(8,128)} custom-call(s32[1]{0:T(128)} %bitcast.6.base_ref, f32[8,40,512]{2,1,0:T(8,128)S(1)} %get-tuple-element.15.all_ref, f32[59,40]{1,0:T(8,128)S(1)} %pad_add_fusion.mix_ref), custom_call_target="tpu_custom_call" | custom-call | tf_op jit(solution)/shard_map/put/pallas_call | solution.py:710
  90.1 0.6 copy.18
  (4 shorter events, 0.0 us)
Async XLA Ops:
  0.6 27.9 %copy-start.1 = (f32[3,1,8,256]{3,2,1,0:T(8,128)S(1)}, f32[3,1,8,256]{3,2,1,0:T(8,128)}, u32[]{:S(2)}) copy-start(f32[3,1,8,256]{3,2,1,0:T(8,128)} %param.14) | copy-start | bytes 73732
  0.7 0.7 copy-start.2
  1.4 0.7 copy-start.5
  2.0 26.5 %copy-start.3 = (bf16[32,256]{1,0:T(8,128)(2,1)S(1)}, bf16[32,256]{1,0:T(8,128)(2,1)}, u32[]{:S(2)}) copy-start(bf16[32,256]{1,0:T(8,128)(2,1)} %constant.34.clone.basis_ref) | copy-start | bytes 49156
  2.0 26.5 %copy-start.4 = (bf16[16,256]{1,0:T(8,128)(2,1)S(1)}, bf16[16,256]{1,0:T(8,128)(2,1)}, u32[]{:S(2)}) copy-start(bf16[16,256]{1,0:T(8,128)(2,1)} %constant.35.clone.basis_t_ref) | copy-start | bytes 24580
  18.3 3.4 %copy-start = (f32[59,32768]{1,0:T(8,128)S(1)}, f32[59,32768]{1,0:T(8,128)}, u32[]{:S(2)}) copy-start(f32[59,32768]{1,0:T(8,128)} %gauss_ref.1) | copy-start | bytes 23199748
  21.7 6.4 %copy-start.6 = (f32[59,40]{1,0:T(8,128)S(1)}, f32[59,40]{1,0:T(8,128)}, u32[]{:S(2)}) copy-start(f32[59,40]{1,0:T(8,128)} %constant.36.clone) | copy-start | bytes 28324

commit v2 on v1

--- a/solution.py
+++ b/solution.py
@@ -95,7 +95,7 @@
     return (((z - dz) & 7) << 2) | ((y - x + dz) & 3)
 
 
-def greet():
+def greet(meanwhile=None):
     cell, view, z, y, x, core = place()
     barrier = pltpu.get_barrier_semaphore()
 
@@ -113,6 +113,8 @@
             signal(server(i, z, y, x, core), view)
     for step in range(1, 8):
         signal(cell, (view + step) & 7)
+    if meanwhile is not None:
+        meanwhile()
     pl.semaphore_wait(barrier, jnp.where(view == 0, 13, 15))
 
 
@@ -166,14 +168,22 @@
     return scales, (qw, qx, qy, qz), norm, inverse, turned
 
 
-def conic_of(consts, scaled):
-    first = [sum(consts[r] * scaled[r][k] for r in range(3)) for k in range(3)]
-    second = [sum(consts[4 + r] * scaled[r][k] for r in range(3)) for k in range(3)]
-    uu = first[0] * first[0] + first[1] * first[1] + first[2] * first[2] + 0.3
-    uv = first[0] * second[0] + first[1] * second[1] + first[2] * second[2]
-    vv = second[0] * second[0] + second[1] * second[1] + second[2] * second[2] + 0.3
-    det = uu * vv - uv * uv
-    return vv / det, -uv / det, uu / det
+PAIRS = ((0, 0), (0, 1), (0, 2), (1, 1), (1, 2), (2, 2))
+
+
+def symmetric(rows):
+    full = dict(zip(PAIRS, rows))
+    return [[full[min(r, t), max(r, t)] for t in range(3)] for r in range(3)]
+
+
+def conic_of(consts, cov):
+    first = [sum(consts[r] * cov[r][t] for r in range(3)) for t in range(3)]
+    second = [sum(consts[4 + r] * cov[r][t] for r in range(3)) for t in range(3)]
+    uu = sum(first[t] * consts[t] for t in range(3)) + 0.3
+    uv = sum(first[t] * consts[4 + t] for t in range(3))
+    vv = sum(second[t] * consts[4 + t] for t in range(3)) + 0.3
+    inverse = 1.0 / (uu * vv - uv * uv)
+    return vv * inverse, -uv * inverse, uu * inverse
 
 
 def log_sigmoid(x):
@@ -181,10 +191,12 @@
 
 
 def ask_kernel(
-    cam_ref, fetch_ref, ids_out, cams_out,
-    row, cams, idv, loc_sem, id_send, id_recv, cam_send, cam_recv,
+    cam_ref, fetch_ref, gauss_ref, ids_out, cams_out, tab_out,
+    tab_sem, row, cams, idv, loc_sem, id_send, id_recv, cam_send, cam_recv,
 ):
     cell, view, z, y, x, core = place()
+    whole = pltpu.make_async_copy(gauss_ref, tab_out, tab_sem)
+    whole.start()
     row[...] = jnp.zeros_like(row)
     row[:, 0:7] = cam_ref[...]
     greet()
@@ -221,22 +233,25 @@
         id_copy(i).wait_send()
     for step in range(1, 8):
         cam_copy(step).wait_send()
-
-
-def project_kernel(
-    ids_ref, cams_ref, gauss_ref, feat_out, params_out, consts_out, tab, got, sem,
-):
-    cell, view, z, y, x, core = place()
-    whole = pltpu.make_async_copy(gauss_ref, tab, sem)
-    whole.start()
+    whole.wait()
+
+
+def project_kernel(ids_ref, cams_ref, tab, brief_out, params_out, consts_out, mix_out, got):
     consts = camera_columns(cams_ref[...])
     lanes = lax.broadcasted_iota(jnp.int32, (8, 128), 1)
     packed = jnp.zeros((8, 128), F32)
-    for k in range(24):
+    for k in range(8):
         packed = jnp.where(lanes == k, consts[k], packed)
     consts_out[...] = packed
+    rows16 = lax.broadcasted_iota(jnp.int32, (16, 128), 0)
+    lanes16 = lax.broadcasted_iota(jnp.int32, (16, 128), 1)
+    mix_out[0:16] = jnp.where((rows16 == lanes16) & (rows16 < 11), 1.0, 0.0)
+    for c in range(3):
+        part = jnp.zeros((8, 128), F32)
+        for k in range(16):
+            part = jnp.where(lanes == 11 + 3 * k + c, consts[8 + k], part)
+        mix_out[16 + 8 * c:24 + 8 * c] = part
     lane = lax.broadcasted_iota(jnp.int32, (59, 128), 1)
-    whole.wait()
 
     def serve(i, carry):
         acc = jnp.zeros((59, 128), F32)
@@ -247,21 +262,15 @@
         got[0:59] = acc
         params_out[i] = got[0:16]
         values = [got[k:k + 1] for k in range(59)]
-        served = requester(i, z, y, x, core)
-        screen_u = sum(consts[r] * values[r] for r in range(3)) + consts[3]
-        screen_v = sum(consts[4 + r] * values[r] for r in range(3)) + (
-            consts[7] - (16 * served + 8).astype(F32)
-        )
         scales, _q, _norm, _inverse, turned = rotation_of(values)
         scaled = [[turned[r][k] * scales[k] for k in range(3)] for r in range(3)]
-        conic_a, conic_b, conic_c = conic_of(consts, scaled)
-        colours = [
-            0.5 + sum(consts[8 + k] * values[11 + 3 * k + c] for k in range(16)) for c in range(3)
-        ]
-        log_opacity = jnp.broadcast_to(log_sigmoid(values[10]), (8, 128))
-        rows = [screen_u, screen_v, conic_a, conic_b, conic_c, log_opacity] + colours
-        for f in range(9):
-            feat_out[i, f] = rows[f]
+        cov = [sum(scaled[r][k] * scaled[t][k] for k in range(3)) for r, t in PAIRS]
+        rows = values[0:3] + cov + [log_sigmoid(values[10])] + [jnp.zeros((1, 128), F32)] * 6
+        brief_out[i, 0:16] = jnp.concatenate(rows, axis=0)
+        for c in range(3):
+            brief_out[i, 16 + 8 * c:24 + 8 * c] = 0.5 + sum(
+                consts[8 + k] * values[11 + 3 * k + c] for k in range(16)
+            )
         return carry
 
     lax.fori_loop(0, 4, serve, 0)
@@ -286,7 +295,18 @@
     return lax.dot_general(a, b, (((0,), (0,)), ((), ())), preferred_element_type=F32)
 
 
-CHUNK = 512
+CHUNK = 1024
+
+
+def mark(list_ref, onehot):
+    low_iota = lax.broadcasted_iota(jnp.int32, (256, 256), 0)
+
+    def one(k, carry):
+        cols = pl.ds(pl.multiple_of(k * 256, 256), 256)
+        onehot[:, cols] = jnp.where(low_iota == (list_ref[:, cols] & 255), 1.0, 0.0).astype(BF16)
+        return carry
+
+    lax.fori_loop(0, 16, one, 0)
 
 
 def composite(
@@ -299,7 +319,6 @@
     table3 = jnp.concatenate(three(table), axis=0).astype(BF16)
     tile_of = lax.broadcasted_iota(jnp.int32, (1, CHUNK), 1) & 7
     in_tile = lax.broadcasted_iota(jnp.int32, (8, CHUNK), 0) == tile_of
-    low_iota = lax.broadcasted_iota(jnp.int32, (256, CHUNK), 0)
     high_iota = lax.broadcasted_iota(jnp.int32, (16, CHUNK), 0)
     zeros_row = jnp.zeros((1, CHUNK), F32)
     image[...] = jnp.zeros_like(image)
@@ -308,9 +327,7 @@
     def forward(k, through):
         cols = pl.ds(pl.multiple_of(k * CHUNK, CHUNK), CHUNK)
         index = list_ref[:, cols]
-        hot = jnp.where(low_iota == (index & 255), 1.0, 0.0).astype(BF16)
-        onehot[:, cols] = hot
-        picked = dot_nn(table3, hot)
+        picked = dot_nn(table3, onehot[:, cols])
         picked = picked[0:144] + picked[144:288] + picked[288:432]
         here = high_iota == (index >> 8)
         rows = [
@@ -338,9 +355,8 @@
         alpha[cols, :] = seen
         for j in range(steps):
             one = seen[8 * j:8 * j + 8]
-            part = through * one
-            weight[pl.ds(pl.multiple_of(k * CHUNK + 8 * j, 8), 8), :] = part
-            through = through - part
+            weight[pl.ds(pl.multiple_of(k * CHUNK + 8 * j, 8), 8), :] = through * one
+            through = through * (1.0 - one)
         part = weight[cols, :]
         part_h = part.astype(BF16)
         part_m = (part - part_h.astype(F32)).astype(BF16)
@@ -350,17 +366,17 @@
             [jnp.where(in_tile, rows[6 + ch], 0.0) for ch in range(3)], axis=0
         )
         high, middle, low = three(masked)
-        stacked = jnp.concatenate([high, middle, low, high, middle, high], axis=0).astype(BF16)
+        stacked = jnp.concatenate([high, middle, high, jnp.zeros((8, CHUNK), F32)], axis=0).astype(BF16)
         colour_rows[:, cols] = stacked
-        image[...] += dot_nn(stacked[0:80], part_h) + dot_nn(stacked[0:80], part_m)
+        image[...] += dot_nn(stacked[0:48], part_h) + dot_nn(stacked[0:48], part_m)
         return through
 
     lax.fori_loop(0, chunks, forward, jnp.ones((8, 256), F32))
-    picture = image[0:24] + image[24:48] + image[48:72]
+    picture = image[0:24] + image[24:48]
     rendered_out[...] = picture
     wrong = picture - target_ref[...]
     high, middle, low = three(wrong)
-    wrong_q = jnp.concatenate([high, high, high, middle, middle, low], axis=0).astype(BF16)
+    wrong_q = jnp.concatenate([high, high, middle, jnp.zeros((8, 256), F32)], axis=0).astype(BF16)
     wrong_w = jnp.concatenate([high, middle], axis=0).astype(BF16)
 
     def backward(step, behind):
@@ -372,7 +388,7 @@
             seen = alpha[at, :]
             gain = value[8 * j:8 * j + 8] - behind
             grad_chunk[8 * j:8 * j + 8, :] = jnp.where(seen < 0.99, weight[at, :] * gain, 0.0)
-            behind = behind + seen * gain
+            behind = behind * (1.0 - seen) + seen * value[8 * j:8 * j + 8]
         grad = grad_chunk[...]
         high, middle, low = three(grad)
         basis_t = basis_t_ref[...]
@@ -403,30 +419,32 @@
         index = list_ref[:, cols]
         here = high_iota == (index >> 8)
         spread = [
-            jnp.where(here, part[f:f + 1], 0.0) for part in three(found) for f in range(9)
+            jnp.where(here, part[f:f + 1], 0.0) for part in three(found)[:2] for f in range(9)
         ]
         spread = jnp.concatenate(spread, axis=0).astype(BF16)
         slot_acc[...] += dot_nt(spread, onehot[:, cols])
         return behind
 
     lax.fori_loop(0, chunks, backward, jnp.zeros((8, 256), F32))
-    total = slot_acc[0:144] + slot_acc[144:288] + slot_acc[288:432]
+    total = slot_acc[0:144] + slot_acc[144:288]
     return total
 
 
 def window_kernel(
-    feat_ref, params_ref, consts_ref, ids_ref, list_ref, target_ref, basis_ref, basis_t_ref,
-    rendered_out, all_out,
-    came, by_server, table, onehot, feats, alpha, weight, weight_h, weight_m, colour_rows, image,
-    grad_chunk, slot_acc, to_server, back, got, gathered,
+    brief_ref, params_ref, consts_ref, ids_ref, list_ref, target_ref, basis_ref, basis_t_ref, mix_ref,
+    rendered_out, grads_out,
+    came, feat, by_server, table, onehot, feats, alpha, weight, weight_h, weight_m, colour_rows,
+    image, grad_chunk, slot_acc, to_server, back, sums, got, gathered, acc,
     out_send, out_recv, in_send, in_recv, back_send, back_recv, own_send, own_recv,
     far_send, far_recv, near_send, near_recv, loc_sem,
 ):
     cell, view, z, y, x, core = place()
-    greet()
-
-    def feature_out(i):
-        source, target = feat_ref.at[i], came.at[i]
+    greet(lambda: mark(list_ref, onehot))
+    consts = [jnp.broadcast_to(consts_ref[:, k:k + 1], (8, 128)) for k in range(8)]
+    down = lambda t: jnp.sum(t, axis=0, keepdims=True)
+
+    def brief_copy(i):
+        source, target = brief_ref.at[i], came.at[i]
         return Or_local(
             i, view,
             lambda: remote(
@@ -436,27 +454,40 @@
             lambda: pltpu.make_async_copy(source, target, out_recv.at[i]),
         )
 
-    def feature_in(step):
+    def feature_copy(step, i):
         who = (view + step) & 7
         return remote(
-            came.at[:, :, who, :], by_server.at[view], in_send.at[step], in_recv.at[step], cell, who
-        )
-
-    for i in range(4):
-        feature_out(i).start()
-    for i in range(4):
-        feature_out(i).wait_recv()
-    for step in range(1, 8):
-        feature_in(step).start()
-    mine = pltpu.make_async_copy(came.at[:, :, view, :], by_server.at[view], loc_sem.at[0])
+            feat.at[i, :, who, :], by_server.at[view, i], in_send.at[step], in_recv.at[step],
+            cell, who,
+        )
+
+    def feature_copies(step):
+        who = (view + step) & 7
+        return remote(
+            feat.at[:, :, who, :], by_server.at[view], in_send.at[step], in_recv.at[step], cell, who
+        )
+
+    for i in (2, 1, 3, 0):
+        brief_copy(i).start()
+    for i in (0, 3, 1, 2):
+        brief_copy(i).wait_recv()
+        rows = [came[i, k:k + 1] for k in range(10)]
+        feat[i, 0] = sum(consts[r] * rows[r] for r in range(3)) + consts[3]
+        feat[i, 1] = sum(consts[4 + r] * rows[r] for r in range(3)) + (
+            consts[7] - (16 * cell + 8).astype(F32)
+        )
+        for f, part in enumerate(conic_of(consts, symmetric(rows[3:9]))):
+            feat[i, 2 + f] = part
+        feat[i, 5] = jnp.broadcast_to(rows[9], (8, 128))
+        for c in range(3):
+            feat[i, 6 + c] = came[i, 16 + 8 * c:24 + 8 * c]
+        for step in range(1, 8):
+            feature_copy(step, i).start()
+    mine = pltpu.make_async_copy(feat.at[:, :, view, :], by_server.at[view], loc_sem.at[0])
     mine.start()
-    for i in range(4):
-        feature_out(i).wait_send()
     mine.wait()
     for step in range(1, 8):
-        feature_in(step).wait_recv()
-    for step in range(1, 8):
-        feature_in(step).wait_send()
+        feature_copies(step).wait_recv()
     for who in range(8):
         for i in range(4):
             row, lanes = 2 * who + i // 2, slice((i % 2) * 128, (i % 2) * 128 + 128)
@@ -482,8 +513,8 @@
             cell, who,
         )
 
-    def grad_own(i):
-        source, target = back.at[i], got.at[i]
+    def sum_copy(i):
+        source, target = sums.at[i], got.at[i]
         return Or_local(
             i, view,
             lambda: remote(
@@ -496,20 +527,14 @@
         grad_back(step).start()
     mine = pltpu.make_async_copy(to_server.at[view], back.at[:, :, view, :], loc_sem.at[1])
     mine.start()
+    acc[...] = jnp.zeros_like(acc)
     mine.wait()
     for step in range(1, 8):
         grad_back(step).wait_recv()
-    for i in range(4):
-        grad_own(i).start()
-    consts = [jnp.broadcast_to(consts_ref[:, k:k + 1], (8, 128)) for k in range(8)]
-    for i in range(4):
-        grad_own(i).wait_recv()
-        values = [params_ref[i, k:k + 1] for k in range(11)]
-        scales, (qw, qx, qy, qz), norm, inverse, turned = rotation_of(values)
-        scaled = [[turned[r][k] * scales[k] for k in range(3)] for r in range(3)]
-        a, b, c = conic_of(consts, scaled)
-        du, dv, da, db, dc, dlog, d0, d1, d2 = [got[i, f] for f in range(9)]
-        down = lambda t: jnp.sum(t, axis=0, keepdims=True)
+    zero = jnp.zeros((1, 128), F32)
+    for i in (2, 1, 3, 0):
+        a, b, c = [feat[i, f] for f in range(2, 5)]
+        du, dv, da, db, dc, dlog = [back[i, f] for f in range(6)]
         position = [down(consts[r] * du + consts[4 + r] * dv) for r in range(3)]
         half = 0.5 * db
         p00 = a * da + b * half
@@ -519,15 +544,21 @@
         s00 = -(p00 * a + p01 * b)
         s01 = -(p00 * b + p01 * c)
         s11 = -(p10 * b + p11 * c)
-        cov = {}
-        for r in range(3):
-            first = consts[r] * s00 + consts[4 + r] * s01
-            second = consts[r] * s01 + consts[4 + r] * s11
-            for t in range(r, 3):
-                cov[r, t] = down(first * consts[t] + second * consts[4 + t])
-                cov[t, r] = cov[r, t]
+        first = [consts[r] * s00 + consts[4 + r] * s01 for r in range(3)]
+        second = [consts[r] * s01 + consts[4 + r] * s11 for r in range(3)]
+        cov = [down(first[r] * consts[t] + second[r] * consts[4 + t]) for r, t in PAIRS]
+        sums[i, 0:16] = jnp.concatenate(position + cov + [down(dlog)] + [zero] * 6, axis=0)
+        for c in range(3):
+            sums[i, 16 + 8 * c:24 + 8 * c] = back[i, 6 + c]
+        sum_copy(i).start()
+    for i in (0, 3, 1, 2):
+        sum_copy(i).wait_recv()
+        values = [params_ref[i, k:k + 1] for k in range(11)]
+        scales, (qw, qx, qy, qz), norm, inverse, turned = rotation_of(values)
+        scaled = [[turned[r][k] * scales[k] for k in range(3)] for r in range(3)]
+        cov = symmetric([got[i, 3 + k:4 + k] for k in range(6)])
         dscaled = [
-            [2.0 * sum(cov[r, t] * scaled[t][k] for t in range(3)) for k in range(3)]
+            [2.0 * sum(cov[r][t] * scaled[t][k] for t in range(3)) for k in range(3)]
             for r in range(3)
         ]
         dlogs = [sum(dscaled[r][k] * scaled[r][k] for r in range(3)) for k in range(3)]
@@ -542,16 +573,13 @@
         ]
         inward = jnp.where(norm > 0.5, qw * qd[0] + qx * qd[1] + qy * qd[2] + qz * qd[3], 0.0)
         dq = [(g - q * inward) * inverse for g, q in zip(qd, (qw, qx, qy, qz))]
-        dlogit = down(dlog) * (1.0 / (1.0 + jnp.exp(values[10])))
+        dlogit = got[i, 9:10] * (1.0 / (1.0 + jnp.exp(values[10])))
         name = ids_ref[i:i + 1].astype(F32)
-        zero = jnp.zeros_like(name)
+        position = [got[i, k:k + 1] for k in range(3)]
         rows = position + dlogs + dq + [dlogit, name] + [zero] * 4
         cols = pl.ds(i * 128, 128)
         gathered[view, 0:16, cols] = jnp.concatenate(rows, axis=0)
-        gathered[view, 16:24, cols] = d0
-        gathered[view, 24:32, cols] = d1
-        gathered[view, 32:40, cols] = d2
-
+        gathered[view, 16:40, cols] = got[i, 16:40]
 
     def far(step):
         who = (view + 2 * step) & 7
@@ -566,58 +594,61 @@
             cell, view ^ 1,
         )
 
+    def far_came(step):
+        which = (view - 2 * step) & 7
+        pltpu.make_async_copy(gathered.at[view], gathered.at[which], far_recv.at[step]).wait()
+        near(step).start()
+        return which
+
+    def near_came(step):
+        which = ((view ^ 1) - 2 * step) & 7
+        pltpu.make_async_copy(gathered.at[view], gathered.at[which], near_recv.at[step]).wait()
+        return which
+
+    base = (view * 4096).astype(F32)
+    low_iota = lax.broadcasted_iota(jnp.int32, (256, 512), 0)
+
+    def deposit(which):
+        block = gathered[which]
+        name = (block[11:12] - base).astype(jnp.int32)
+        hot = jnp.where(low_iota == (name & 255), 1.0, 0.0).astype(BF16)
+        row = name >> 8
+        parts = jnp.concatenate(three(block)[:2], axis=0)
+        spread = [jnp.where(row == h, parts, 0.0).astype(BF16) for h in range(16)]
+        acc[...] += dot_nt(jnp.concatenate(spread, axis=0), hot)
+
     for step in (2, 1, 3):
         far(step).start()
     near(0).start()
+    deposit(view)
+    deposit(near_came(0))
+    one, three_ = far_came(1), far_came(3)
+    deposit(one)
+    two = far_came(2)
+    deposit(three_)
+    deposit(two)
     for step in (1, 3, 2):
-        which = (view - 2 * step) & 7
-        pltpu.make_async_copy(gathered.at[view], gathered.at[which], far_recv.at[step]).wait()
-        near(step).start()
-    for step in range(4):
-        which = ((view ^ 1) - 2 * step) & 7
-        pltpu.make_async_copy(gathered.at[view], gathered.at[which], near_recv.at[step]).wait()
+        deposit(near_came(step))
+
+    mix = mix_ref[...].T[0:59]
+    for h in range(16):
+        at = 80 * h
+        grads_out[:, h * 256:(h + 1) * 256] = jnp.dot(
+            mix, acc[at:at + 40] + acc[at + 40:at + 80],
+            precision=lax.Precision.HIGHEST, preferred_element_type=F32,
+        )
+    for i in range(4):
+        brief_copy(i).wait_send()
+    for step in range(1, 8):
+        feature_copies(step).wait_send()
     for step in range(1, 8):
         grad_back(step).wait_send()
     for i in range(4):
-        grad_own(i).wait_send()
+        sum_copy(i).wait_send()
     for step in (1, 2, 3):
         far(step).wait_send()
     for step in range(4):
         near(step).wait_send()
-    all_out[...] = gathered[...]
-
-
-def place_kernel(base_ref, all_ref, mix_ref, out_ref, acc):
-    base = base_ref[0]
-    low_iota = lax.broadcasted_iota(jnp.int32, (256, 512), 0)
-    acc[...] = jnp.zeros_like(acc)
-
-    def one(source, carry):
-        block = all_ref[source]
-        name = block[11:12].astype(jnp.int32) - base
-        hot = jnp.where(low_iota == (name & 255), 1.0, 0.0).astype(BF16)
-        high = name >> 8
-        parts = jnp.concatenate(three(block), axis=0)
-        spread = jnp.concatenate(
-            [
-                jnp.concatenate(
-                    [jnp.where(high == h, parts, 0.0), jnp.where(high == h + 1, parts, 0.0)], axis=0
-                ).astype(BF16)
-                for h in range(0, 16, 2)
-            ],
-            axis=0,
-        )
-        acc[...] += dot_nt(spread, hot)
-        return carry
-
-    lax.fori_loop(0, 8, one, 0)
-    mix = mix_ref[...]
-    for h in range(16):
-        at = 120 * h
-        found = acc[at:at + 40] + acc[at + 40:at + 80] + acc[at + 80:at + 120]
-        out_ref[:, h * 256:(h + 1) * 256] = jnp.dot(
-            mix, found, precision=lax.Precision.HIGHEST, preferred_element_type=F32
-        )
 
 
 def pixel_basis():
@@ -640,45 +671,47 @@
     return jax.ShapeDtypeStruct(dims, dtype)
 
 
-def ask(camera, ids):
+def ask(camera, ids, gaussians):
     return pl.pallas_call(
         ask_kernel,
-        out_shape=(shape(4, 128, dtype=jnp.int32), shape(8, 128)),
-        in_specs=[VM, VM],
-        out_specs=(VM, VM),
+        out_shape=(shape(4, 128, dtype=jnp.int32), shape(8, 128), shape(59, 32768)),
+        in_specs=[VM, VM, pl.BlockSpec(memory_space=pltpu.HBM)],
+        out_specs=(VM, VM, pl.BlockSpec(memory_space=pl.ANY)),
         scratch_shapes=[
+            DMA,
             pltpu.VMEM((1, 128), F32),
             pltpu.VMEM((8, 128), F32),
             pltpu.VMEM((4, 128), jnp.int32),
             DMA, DMA((4,)), DMA((4,)), DMA((8,)), DMA((8,)),
         ],
         compiler_params=pltpu.CompilerParams(
-            collective_id=0, has_side_effects=True, vmem_limit_bytes=2 * MIB
+            collective_id=0, has_side_effects=True, vmem_limit_bytes=44 * MIB
         ),
         name="ask",
-    )(camera, ids)
+    )(camera, ids, gaussians)
 
 
 def project(ids, cams, gaussians):
     return pl.pallas_call(
         project_kernel,
-        out_shape=(shape(4, 9, 8, 128), shape(4, 16, 128), shape(8, 128)),
-        in_specs=[SM, VM, pl.BlockSpec(memory_space=pl.ANY)],
-        out_specs=(VM, VM, VM),
-        scratch_shapes=[pltpu.VMEM((59, 32768), F32), pltpu.VMEM((64, 128), F32), DMA],
+        out_shape=(shape(4, 40, 128), shape(4, 16, 128), shape(8, 128), shape(40, 128)),
+        in_specs=[SM, VM, VM],
+        out_specs=(VM, VM, VM, VM),
+        scratch_shapes=[pltpu.VMEM((64, 128), F32)],
         compiler_params=pltpu.CompilerParams(vmem_limit_bytes=16 * MIB),
         name="project",
     )(ids, cams, gaussians)
 
 
-def window(feat, params, consts, ids, listed, target):
+def window(brief, params, consts, ids, listed, target, mix):
     wide, tall = pixel_basis()
     return pl.pallas_call(
         window_kernel,
-        out_shape=(shape(24, 256), shape(8, 40, 512)),
-        in_specs=[VM] * 8,
+        out_shape=(shape(24, 256), shape(59, 4096)),
+        in_specs=[VM] * 9,
         out_specs=(VM, VM),
         scratch_shapes=[
+            pltpu.VMEM((4, 40, 128), F32),
             pltpu.VMEM((4, 9, 8, 128), F32),
             pltpu.VMEM((8, 4, 9, 128), F32),
             pltpu.VMEM((9, 16, 256), F32),
@@ -688,14 +721,16 @@
             pltpu.VMEM((4096, 256), F32),
             pltpu.VMEM((4096, 256), BF16),
             pltpu.VMEM((4096, 256), BF16),
-            pltpu.VMEM((144, 4096), BF16),
-            pltpu.VMEM((80, 256), F32),
+            pltpu.VMEM((80, 4096), BF16),
+            pltpu.VMEM((48, 256), F32),
             pltpu.VMEM((CHUNK, 256), F32),
-            pltpu.VMEM((432, 256), F32),
+            pltpu.VMEM((288, 256), F32),
             pltpu.VMEM((8, 4, 9, 128), F32),
             pltpu.VMEM((4, 9, 8, 128), F32),
-            pltpu.VMEM((4, 9, 8, 128), F32),
+            pltpu.VMEM((4, 40, 128), F32),
+            pltpu.VMEM((4, 40, 128), F32),
             pltpu.VMEM((8, 40, 512), F32),
+            pltpu.VMEM((1280, 256), F32),
             DMA((4,)), DMA((4,)), DMA((8,)), DMA((8,)), DMA((8,)), DMA((8,)), DMA((4,)), DMA((4,)),
             DMA((4,)), DMA((4,)), DMA((4,)), DMA((4,)), DMA((2,)),
         ],
@@ -703,26 +738,7 @@
             collective_id=1, has_side_effects=True, vmem_limit_bytes=48 * MIB
         ),
         name="window",
-    )(feat, params, consts, ids, listed, target, wide, tall)
-
-
-def put(base, everything, mix):
-    return pl.pallas_call(
-        place_kernel,
-        out_shape=shape(59, 4096),
-        in_specs=[SM, VM, VM],
-        out_specs=VM,
-        scratch_shapes=[pltpu.VMEM((1920, 256), F32)],
-        compiler_params=pltpu.CompilerParams(vmem_limit_bytes=32 * MIB),
-        name="put",
-    )(base, everything, mix)
-
-
-def mixing(consts):
-    harmonics = consts[:, 8:24].T
-    spread = harmonics[:, None, None, :] * jnp.eye(3, dtype=F32)[None, :, :, None]
-    colour = jnp.pad(spread.reshape(48, 24), ((11, 0), (16, 0)))
-    return colour + jnp.asarray(np.eye(59, 40) * (np.arange(59) < 11)[:, None], F32)
+    )(brief, params, consts, ids, listed, target, wide, tall, mix)
 
 
 def slots_of(entries):
@@ -738,11 +754,9 @@
     live = jnp.arange(512, dtype=jnp.int32)[:, None] < lengths[None, :]
     listed = jnp.where(live, slots_of(tile_lists[0]).T, -1).reshape(1, 4096)
     target = target_image.reshape(24, 256)
-    ids, cams = ask(cameras, fetch_ids[0])
-    feat, params, consts = project(ids, cams, gaussians)
-    picture, everything = window(feat, params, consts, ids, listed, target)
-    base = (lax.axis_index("view") * 4096).astype(jnp.int32).reshape(1)
-    param_grads = put(base, everything, mixing(consts))
+    ids, cams, table = ask(cameras, fetch_ids[0], gaussians)
+    brief, params, consts, mix = project(ids, cams, table)
+    picture, param_grads = window(brief, params, consts, ids, listed, target, mix)
     return picture.reshape(3, 1, 8, 256), param_grads
 
 

time: 91 us -> 75.5 us (0.83)
  Pallas kernels: 83.1 us -> 71 us
  local copies, waits for them, and re-layouts: 5.91 us -> 3.26 us
    pallas_call x3 -> x2, Pallas kernels: 67.7 us -> 55.5 us  [the longest x1 49.8 us: window(): pl.pallas_call(window_kernel, out_shape=(shape(24, 256), shape(59, 4096))...]
    unnamed x15 -> x16, local copies, waits for them, and re-layouts: 5.37 us -> 2.97 us
where the time goes in v2:
time: 75.5 us; the launch traced here: 75.1 us
  Pallas kernels  71 us (94%)
  local copies, waits for them, and re-layouts  3.26 us (4%)
    pallas_call x1, Pallas kernels, window(): pl.pallas_call(window_kernel, out_shape=(shape(24, 256), shape(59, 4096))...  49.8 us
    pallas_call x1, Pallas kernels, ask(): pl.pallas_call(ask_kernel, out_shape=(shape(4, 128, dtype=jnp.int32), sha...  15.5 us
    pallas_call x1, Pallas kernels, project(): pl.pallas_call(project_kernel, out_shape=(shape(4, 40, 128), shape(4, 16,...  5.67 us
    unnamed x16, local copies, waits for them, and re-layouts  2.97 us

profile of v2, /device:TPU:1, one launch (start us, length us, event | category | flops | bytes accessed | tf_op | source)
XLA Modules:
  0.0 75.1 jit_solution(6454651888388381947)
XLA Ops:
  0.6 0.0 copy-start.1
  0.6 0.7 copy-done.1
  1.4 0.0 copy-start.4
  1.4 0.7 copy-done.4
  2.0 0.0 copy-start.5
  2.0 0.0 copy-start.6
  2.0 0.0 copy-start
  2.0 0.0 copy-start.2
  2.0 0.0 copy-start.3
  2.0 15.5 %ask.1 = (s32[4,128]{1,0:T(4,128)S(1)}, f32[8,128]{1,0:T(8,128)S(1)}, f32[59,32768]{1,0:T(8,128)S(1)}) custom-call(f32[1,7]{1,0:T(1,128)S(1)} %copy-done.4, s32[32,128]{1,0:T(8,128)S(1)} %bitcast.11, f32[59,32768]{1,0:T(8,128)} %gauss_ref.1), custom_call_target="tpu_custom_call" | custom-call | tf_op jit(solution)/shard_map/ask/pallas_call | solution.py:675
  17.6 5.7 %project.1 = (f32[4,40,128]{2,1,0:T(8,128)S(1)}, f32[4,16,128]{2,1,0:T(8,128)S(1)}, f32[8,128]{1,0:T(8,128)S(1)}, f32[40,128]{1,0:T(8,128)S(1)}) custom-call(s32[4,128]{1,0:T(4,128)S(1)} %get-tuple-element.11.ids_ref, f32[8,128]{1,0:T(8,128)S(1)} %get-tuple-element.12.cams_ref, f32[59,32768]{1,0:T(8,128)S(1)} %get-tuple-element.13.tab), custom_call_target="tpu_custom_call" | custom-call | tf_op jit(solution)/shard_map/project/pallas_call | solution.py:695
  23.2 0.0 copy-done.5
  23.3 0.0 copy-done.6
  23.3 0.1 bitcast_select_fusion
  23.3 0.1 copy.12
  23.5 0.2 reshape.30.list_ref
  23.6 0.0 copy-done
  23.7 0.0 copy-done.2
  23.7 0.0 copy-done.3
  23.7 49.8 %window.1 = (f32[24,256]{1,0:T(8,128)S(1)}, f32[59,4096]{1,0:T(8,128)S(1)}) custom-call(f32[4,40,128]{2,1,0:T(8,128)S(1)} %get-tuple-element.14.brief_ref, f32[4,16,128]{2,1,0:T(8,128)S(1)} %get-tuple-element.15.params_ref, f32[8,128]{1,0:T(8,128)S(1)} %get-tuple-element.16.consts_ref, s32[4,128]{1,0:T(4,128)S(1)} %get-tuple-element.11.ids_ref, ...), custom_call_target="tpu_custom_call" | custom-call | tf_op jit(solution)/shard_map/window/pallas_call | solution.py:708
  73.5 0.6 copy.16
  74.1 1.0 %copy.17 = f32[59,4096]{1,0:T(8,128)} copy(f32[59,4096]{1,0:T(8,128)S(1)} %get-tuple-element.27) | data formatting | bytes 1933312
Async XLA Ops:
  0.6 0.7 copy-start.1
  1.4 0.7 copy-start.4
  2.0 21.2 %copy-start.5 = (s32[1,8,512]{2,1,0:T(8,128)S(1)}, s32[1,8,512]{2,1,0:T(8,128)}, u32[]{:S(2)}) copy-start(s32[1,8,512]{2,1,0:T(8,128)} %param.11) | copy-start | bytes 49156
  2.0 21.2 %copy-start.6 = (s32[8]{0:T(128)S(1)}, s32[8]{0:T(128)}, u32[]{:S(2)}) copy-start(s32[8]{0:T(128)} %param.12) | copy-start | bytes 100
  2.0 21.6 %copy-start = (f32[3,1,8,256]{3,2,1,0:T(8,128)S(1)}, f32[3,1,8,256]{3,2,1,0:T(8,128)}, u32[]{:S(2)}) copy-start(f32[3,1,8,256]{3,2,1,0:T(8,128)} %param.13) | copy-start | bytes 73732
  2.0 21.6 %copy-start.2 = (bf16[32,256]{1,0:T(8,128)(2,1)S(1)}, bf16[32,256]{1,0:T(8,128)(2,1)}, u32[]{:S(2)}) copy-start(bf16[32,256]{1,0:T(8,128)(2,1)} %constant.24.clone.basis_ref) | copy-start | bytes 49156
  2.0 21.7 %copy-start.3 = (bf16[16,256]{1,0:T(8,128)(2,1)S(1)}, bf16[16,256]{1,0:T(8,128)(2,1)}, u32[]{:S(2)}) copy-start(bf16[16,256]{1,0:T(8,128)(2,1)} %constant.25.clone.basis_t_ref) | copy-start | bytes 24580

commit v3 on v2

--- a/solution.py
+++ b/solution.py
@@ -95,27 +95,53 @@
     return (((z - dz) & 7) << 2) | ((y - x + dz) & 3)
 
 
-def greet(meanwhile=None):
+def hello(where, who):
+    pl.semaphore_signal(
+        pltpu.get_barrier_semaphore(), inc=1, device_id=(where, who), device_id_type=MESH
+    )
+
+
+def greet_ask():
     cell, view, z, y, x, core = place()
-    barrier = pltpu.get_barrier_semaphore()
-
-    def signal(where, who):
-        pl.semaphore_signal(barrier, inc=1, device_id=(where, who), device_id_type=MESH)
-
     for i in range(4):
         if i == 0:
             @pl.when(view != 0)
             def _():
-                signal(requester(0, z, y, x, core), view)
-                signal(server(0, z, y, x, core), view)
+                hello(requester(0, z, y, x, core), view)
         else:
-            signal(requester(i, z, y, x, core), view)
-            signal(server(i, z, y, x, core), view)
+            hello(requester(i, z, y, x, core), view)
     for step in range(1, 8):
-        signal(cell, (view + step) & 7)
-    if meanwhile is not None:
-        meanwhile()
-    pl.semaphore_wait(barrier, jnp.where(view == 0, 13, 15))
+        hello(cell, (view + step) & 7)
+    pl.semaphore_wait(pltpu.get_barrier_semaphore(), jnp.where(view == 0, 10, 11))
+
+
+OFFSETS = [(dz, dy) for dz in (4, 3, 5, 2, 6, 1, 7, 0) for dy in (2, 1, 3, 0)]
+
+
+def owner_at(offset, z, y):
+    dz, dy = offset
+    return (((z - dz) & 7) << 2) | ((y - dy) & 3), (((dy + dz) & 3) << 1) | (dz & 1), dz >> 1
+
+
+def greet_window(meanwhile):
+    cell, view, z, y, x, core = place()
+    for offset in OFFSETS:
+        owner, who, _i = owner_at(offset, z, y)
+        if offset == (0, 0):
+            @pl.when(view != 0)
+            def _():
+                hello(owner, who)
+        else:
+            hello(owner, who)
+    for step in range(1, 4):
+        hello(cell, (view + 2 * step) & 7)
+    hello(cell, view ^ 1)
+    meanwhile()
+    pl.semaphore_wait(pltpu.get_barrier_semaphore(), jnp.where(view == 0, 35, 36))
+
+
+def slot_window(ref, owner):
+    return ref.at[:, owner >> 1, pl.ds(pl.multiple_of((owner & 1) * 128, 128), 128)]
 
 
 class Or_local:
@@ -199,7 +225,7 @@
     whole.start()
     row[...] = jnp.zeros_like(row)
     row[:, 0:7] = cam_ref[...]
-    greet()
+    greet_ask()
 
     def id_copy(i):
         owner = server(i, z, y, x, core)
@@ -236,7 +262,8 @@
     whole.wait()
 
 
-def project_kernel(ids_ref, cams_ref, tab, brief_out, params_out, consts_out, mix_out, got):
+def project_kernel(ids_ref, cams_ref, tab, feat_out, params_out, consts_out, mix_out, got):
+    cell, view, z, y, x, core = place()
     consts = camera_columns(cams_ref[...])
     lanes = lax.broadcasted_iota(jnp.int32, (8, 128), 1)
     packed = jnp.zeros((8, 128), F32)
@@ -265,10 +292,16 @@
         scales, _q, _norm, _inverse, turned = rotation_of(values)
         scaled = [[turned[r][k] * scales[k] for k in range(3)] for r in range(3)]
         cov = [sum(scaled[r][k] * scaled[t][k] for k in range(3)) for r, t in PAIRS]
-        rows = values[0:3] + cov + [log_sigmoid(values[10])] + [jnp.zeros((1, 128), F32)] * 6
-        brief_out[i, 0:16] = jnp.concatenate(rows, axis=0)
+        served = requester(i, z, y, x, core)
+        feat_out[i, 0] = sum(consts[r] * values[r] for r in range(3)) + consts[3]
+        feat_out[i, 1] = sum(consts[4 + r] * values[r] for r in range(3)) + (
+            consts[7] - (16 * served + 8).astype(F32)
+        )
+        for f, part in enumerate(conic_of(consts, symmetric(cov))):
+            feat_out[i, 2 + f] = part
+        feat_out[i, 5] = jnp.broadcast_to(log_sigmoid(values[10]), (8, 128))
         for c in range(3):
-            brief_out[i, 16 + 8 * c:24 + 8 * c] = 0.5 + sum(
+            feat_out[i, 6 + c] = 0.5 + sum(
                 consts[8 + k] * values[11 + 3 * k + c] for k in range(16)
             )
         return carry
@@ -295,7 +328,7 @@
     return lax.dot_general(a, b, (((0,), (0,)), ((), ())), preferred_element_type=F32)
 
 
-CHUNK = 1024
+CHUNK = 2048
 
 
 def mark(list_ref, onehot):
@@ -431,110 +464,88 @@
 
 
 def window_kernel(
-    brief_ref, params_ref, consts_ref, ids_ref, list_ref, target_ref, basis_ref, basis_t_ref, mix_ref,
+    feat_ref, params_ref, consts_ref, ids_ref, list_ref, target_ref, basis_ref, basis_t_ref, mix_ref,
     rendered_out, grads_out,
-    came, feat, by_server, table, onehot, feats, alpha, weight, weight_h, weight_m, colour_rows,
-    image, grad_chunk, slot_acc, to_server, back, sums, got, gathered, acc,
-    out_send, out_recv, in_send, in_recv, back_send, back_recv, own_send, own_recv,
-    far_send, far_recv, near_send, near_recv, loc_sem,
+    table, onehot, feats, alpha, weight, weight_h, weight_m, colour_rows,
+    image, grad_chunk, slot_acc, leaving, got, gathered, acc,
+    f_send, f_recv, b_send, b_recv, far_send, far_recv, near_send, near_recv,
 ):
     cell, view, z, y, x, core = place()
-    greet(lambda: mark(list_ref, onehot))
+    greet_window(lambda: mark(list_ref, onehot))
     consts = [jnp.broadcast_to(consts_ref[:, k:k + 1], (8, 128)) for k in range(8)]
     down = lambda t: jnp.sum(t, axis=0, keepdims=True)
 
-    def brief_copy(i):
-        source, target = brief_ref.at[i], came.at[i]
+    def feature_copy(i, v):
+        source, target = feat_ref.at[i, :, v, :], slot_window(table, cell)
         return Or_local(
-            i, view,
+            i + v, view,
             lambda: remote(
-                source, target, out_send.at[i], out_recv.at[i],
-                requester(i, z, y, x, core), view,
+                source, target, f_send.at[i * 8 + v], f_recv.at[cell],
+                requester(i, z, y, x, core), v,
             ),
-            lambda: pltpu.make_async_copy(source, target, out_recv.at[i]),
-        )
-
-    def feature_copy(step, i):
-        who = (view + step) & 7
-        return remote(
-            feat.at[i, :, who, :], by_server.at[view, i], in_send.at[step], in_recv.at[step],
-            cell, who,
-        )
-
-    def feature_copies(step):
-        who = (view + step) & 7
-        return remote(
-            feat.at[:, :, who, :], by_server.at[view], in_send.at[step], in_recv.at[step], cell, who
+            lambda: pltpu.make_async_copy(source, target, f_recv.at[cell]),
         )
 
     for i in (2, 1, 3, 0):
-        brief_copy(i).start()
-    for i in (0, 3, 1, 2):
-        brief_copy(i).wait_recv()
-        rows = [came[i, k:k + 1] for k in range(10)]
-        feat[i, 0] = sum(consts[r] * rows[r] for r in range(3)) + consts[3]
-        feat[i, 1] = sum(consts[4 + r] * rows[r] for r in range(3)) + (
-            consts[7] - (16 * cell + 8).astype(F32)
-        )
-        for f, part in enumerate(conic_of(consts, symmetric(rows[3:9]))):
-            feat[i, 2 + f] = part
-        feat[i, 5] = jnp.broadcast_to(rows[9], (8, 128))
-        for c in range(3):
-            feat[i, 6 + c] = came[i, 16 + 8 * c:24 + 8 * c]
-        for step in range(1, 8):
-            feature_copy(step, i).start()
-    mine = pltpu.make_async_copy(feat.at[:, :, view, :], by_server.at[view], loc_sem.at[0])
-    mine.start()
-    mine.wait()
-    for step in range(1, 8):
-        feature_copies(step).wait_recv()
-    for who in range(8):
-        for i in range(4):
-            row, lanes = 2 * who + i // 2, slice((i % 2) * 128, (i % 2) * 128 + 128)
-            for f in range(9):
-                table[f, row:row + 1, lanes] = by_server[who, i, f:f + 1]
+        for v in range(8):
+            feature_copy(i, v).start()
+
+    def arrived(owner, carry):
+        pltpu.make_async_copy(
+            feat_ref.at[0, :, 0, :], slot_window(table, owner), f_recv.at[owner]
+        ).wait()
+        return carry
+
+    lax.fori_loop(0, 32, arrived, 0)
 
     total = composite(
         table, list_ref, target_ref, basis_ref, basis_t_ref, rendered_out,
         onehot, feats, alpha, weight, weight_h, weight_m, colour_rows, image, grad_chunk, slot_acc,
     )
-
-    slot_acc[0:144] = total
-    for who in range(8):
-        for i in range(4):
-            row, lanes = 2 * who + i // 2, slice((i % 2) * 128, (i % 2) * 128 + 128)
-            for f in range(9):
-                to_server[who, i, f:f + 1] = slot_acc[16 * f + row:16 * f + row + 1, lanes]
-
-    def grad_back(step):
-        who = (view + step) & 7
+    leaving[...] = total.reshape(9, 16, 256)
+
+    def grad_copy(n):
+        owner, who, i = owner_at(OFFSETS[n], z, y)
+        source, target = slot_window(leaving, owner), got.at[i, :, view, :]
+        return Or_local(
+            31 - n, view,
+            lambda: remote(source, target, b_send.at[n], b_recv.at[i * 8 + view], owner, who),
+            lambda: pltpu.make_async_copy(source, target, b_recv.at[i * 8 + view]),
+        )
+
+    for n in range(32):
+        grad_copy(n).start()
+    acc[...] = jnp.zeros_like(acc)
+
+    def far(step, i):
+        who = (view + 2 * step) & 7
         return remote(
-            to_server.at[who], back.at[:, :, view, :], back_send.at[step], back_recv.at[step],
+            gathered.at[view, i], gathered.at[view, i], far_send.at[step, i], far_recv.at[step, i],
             cell, who,
         )
 
-    def sum_copy(i):
-        source, target = sums.at[i], got.at[i]
-        return Or_local(
-            i, view,
-            lambda: remote(
-                source, target, own_send.at[i], own_recv.at[i], server(i, z, y, x, core), view
-            ),
-            lambda: pltpu.make_async_copy(source, target, own_recv.at[i]),
-        )
-
-    for step in range(1, 8):
-        grad_back(step).start()
-    mine = pltpu.make_async_copy(to_server.at[view], back.at[:, :, view, :], loc_sem.at[1])
-    mine.start()
-    acc[...] = jnp.zeros_like(acc)
-    mine.wait()
-    for step in range(1, 8):
-        grad_back(step).wait_recv()
+    def near(step, i):
+        which = (view - 2 * step) & 7
+        return remote(
+            gathered.at[which, i], gathered.at[which, i],
+            near_send.at[step, i], near_recv.at[step, i], cell, view ^ 1,
+        )
+
+    values = [
+        jnp.concatenate([params_ref[i, k:k + 1] for i in range(4)], axis=1) for k in range(11)
+    ]
+    all_scales, all_turns, all_norm, all_inverse, turned = rotation_of(values)
+    all_scaled = [turned[r][k] * all_scales[k] for r in range(3) for k in range(3)]
+    all_faint = 1.0 / (1.0 + jnp.exp(values[10]))
     zero = jnp.zeros((1, 128), F32)
-    for i in (2, 1, 3, 0):
-        a, b, c = [feat[i, f] for f in range(2, 5)]
-        du, dv, da, db, dc, dlog = [back[i, f] for f in range(6)]
+    order = (0, 3, 1, 2)
+    for i in order:
+        for v in range(8):
+            pltpu.make_async_copy(
+                slot_window(leaving, cell), got.at[i, :, v, :], b_recv.at[i * 8 + v]
+            ).wait()
+        a, b, c = [feat_ref[i, f] for f in range(2, 5)]
+        du, dv, da, db, dc, dlog = [got[i, f] for f in range(6)]
         position = [down(consts[r] * du + consts[4 + r] * dv) for r in range(3)]
         half = 0.5 * db
         p00 = a * da + b * half
@@ -547,16 +558,13 @@
         first = [consts[r] * s00 + consts[4 + r] * s01 for r in range(3)]
         second = [consts[r] * s01 + consts[4 + r] * s11 for r in range(3)]
         cov = [down(first[r] * consts[t] + second[r] * consts[4 + t]) for r, t in PAIRS]
-        sums[i, 0:16] = jnp.concatenate(position + cov + [down(dlog)] + [zero] * 6, axis=0)
-        for c in range(3):
-            sums[i, 16 + 8 * c:24 + 8 * c] = back[i, 6 + c]
-        sum_copy(i).start()
-    for i in (0, 3, 1, 2):
-        sum_copy(i).wait_recv()
-        values = [params_ref[i, k:k + 1] for k in range(11)]
-        scales, (qw, qx, qy, qz), norm, inverse, turned = rotation_of(values)
-        scaled = [[turned[r][k] * scales[k] for k in range(3)] for r in range(3)]
-        cov = symmetric([got[i, 3 + k:4 + k] for k in range(6)])
+        lanes = slice(128 * i, 128 * i + 128)
+        scales, (qw, qx, qy, qz), scaled = [
+            [t[:, lanes] for t in group] for group in (all_scales, all_turns, all_scaled)
+        ]
+        scaled = [scaled[3 * r:3 * r + 3] for r in range(3)]
+        inverse, faint = all_inverse[:, lanes], all_faint[:, lanes]
+        cov = symmetric(cov)
         dscaled = [
             [2.0 * sum(cov[r][t] * scaled[t][k] for t in range(3)) for k in range(3)]
             for r in range(3)
@@ -571,45 +579,38 @@
             2.0 * (qx * (e01 + e10) + qw * (e02 - e20) + qz * (e12 + e21) - 2.0 * qy * (e00 + e22)),
             2.0 * (qw * (e10 - e01) + qx * (e02 + e20) + qy * (e12 + e21) - 2.0 * qz * (e00 + e11)),
         ]
-        inward = jnp.where(norm > 0.5, qw * qd[0] + qx * qd[1] + qy * qd[2] + qz * qd[3], 0.0)
+        inward = jnp.where(all_norm[:, lanes] > 0.5, qw * qd[0] + qx * qd[1] + qy * qd[2] + qz * qd[3], 0.0)
         dq = [(g - q * inward) * inverse for g, q in zip(qd, (qw, qx, qy, qz))]
-        dlogit = got[i, 9:10] * (1.0 / (1.0 + jnp.exp(values[10])))
+        dlogit = down(dlog) * faint
         name = ids_ref[i:i + 1].astype(F32)
-        position = [got[i, k:k + 1] for k in range(3)]
         rows = position + dlogs + dq + [dlogit, name] + [zero] * 4
-        cols = pl.ds(i * 128, 128)
-        gathered[view, 0:16, cols] = jnp.concatenate(rows, axis=0)
-        gathered[view, 16:40, cols] = got[i, 16:40]
-
-    def far(step):
-        who = (view + 2 * step) & 7
-        return remote(
-            gathered.at[view], gathered.at[view], far_send.at[step], far_recv.at[step], cell, who
-        )
-
-    def near(step):
+        gathered[view, i, 0:16] = jnp.concatenate(rows, axis=0)
+        for ch in range(3):
+            gathered[view, i, 16 + 8 * ch:24 + 8 * ch] = got[i, 6 + ch]
+        for step in (2, 1, 3):
+            far(step, i).start()
+        near(0, i).start()
+
+    def far_came(step, i):
         which = (view - 2 * step) & 7
-        return remote(
-            gathered.at[which], gathered.at[which], near_send.at[step], near_recv.at[step],
-            cell, view ^ 1,
-        )
-
-    def far_came(step):
-        which = (view - 2 * step) & 7
-        pltpu.make_async_copy(gathered.at[view], gathered.at[which], far_recv.at[step]).wait()
-        near(step).start()
-        return which
+        pltpu.make_async_copy(
+            gathered.at[view, i], gathered.at[which, i], far_recv.at[step, i]
+        ).wait()
+        near(step, i).start()
 
     def near_came(step):
         which = ((view ^ 1) - 2 * step) & 7
-        pltpu.make_async_copy(gathered.at[view], gathered.at[which], near_recv.at[step]).wait()
+        for i in order:
+            pltpu.make_async_copy(
+                gathered.at[view, i], gathered.at[which, i], near_recv.at[step, i]
+            ).wait()
         return which
 
     base = (view * 4096).astype(F32)
     low_iota = lax.broadcasted_iota(jnp.int32, (256, 512), 0)
 
     def deposit(which):
-        block = gathered[which]
+        block = jnp.concatenate([gathered[which, i] for i in range(4)], axis=1)
         name = (block[11:12] - base).astype(jnp.int32)
         hot = jnp.where(low_iota == (name & 255), 1.0, 0.0).astype(BF16)
         row = name >> 8
@@ -617,16 +618,15 @@
         spread = [jnp.where(row == h, parts, 0.0).astype(BF16) for h in range(16)]
         acc[...] += dot_nt(jnp.concatenate(spread, axis=0), hot)
 
-    for step in (2, 1, 3):
-        far(step).start()
-    near(0).start()
     deposit(view)
+    for i in order:
+        far_came(1, i)
+        far_came(3, i)
     deposit(near_came(0))
-    one, three_ = far_came(1), far_came(3)
-    deposit(one)
-    two = far_came(2)
-    deposit(three_)
-    deposit(two)
+    for i in order:
+        far_came(2, i)
+    for step in (1, 3, 2):
+        deposit((view - 2 * step) & 7)
     for step in (1, 3, 2):
         deposit(near_came(step))
 
@@ -638,17 +638,15 @@
             precision=lax.Precision.HIGHEST, preferred_element_type=F32,
         )
     for i in range(4):
-        brief_copy(i).wait_send()
-    for step in range(1, 8):
-        feature_copies(step).wait_send()
-    for step in range(1, 8):
-        grad_back(step).wait_send()
+        for v in range(8):
+            feature_copy(i, v).wait_send()
+    for n in range(32):
+        grad_copy(n).wait_send()
     for i in range(4):
-        sum_copy(i).wait_send()
-    for step in (1, 2, 3):
-        far(step).wait_send()
-    for step in range(4):
-        near(step).wait_send()
+        for step in (1, 2, 3):
+            far(step, i).wait_send()
+        for step in range(4):
+            near(step, i).wait_send()
 
 
 def pixel_basis():
@@ -694,7 +692,7 @@
 def project(ids, cams, gaussians):
     return pl.pallas_call(
         project_kernel,
-        out_shape=(shape(4, 40, 128), shape(4, 16, 128), shape(8, 128), shape(40, 128)),
+        out_shape=(shape(4, 9, 8, 128), shape(4, 16, 128), shape(8, 128), shape(40, 128)),
         in_specs=[SM, VM, VM],
         out_specs=(VM, VM, VM, VM),
         scratch_shapes=[pltpu.VMEM((64, 128), F32)],
@@ -703,7 +701,7 @@
     )(ids, cams, gaussians)
 
 
-def window(brief, params, consts, ids, listed, target, mix):
+def window(feat, params, consts, ids, listed, target, mix):
     wide, tall = pixel_basis()
     return pl.pallas_call(
         window_kernel,
@@ -711,9 +709,6 @@
         in_specs=[VM] * 9,
         out_specs=(VM, VM),
         scratch_shapes=[
-            pltpu.VMEM((4, 40, 128), F32),
-            pltpu.VMEM((4, 9, 8, 128), F32),
-            pltpu.VMEM((8, 4, 9, 128), F32),
             pltpu.VMEM((9, 16, 256), F32),
             pltpu.VMEM((256, 4096), BF16),
             pltpu.VMEM((8, 4096), F32),
@@ -725,38 +720,27 @@
             pltpu.VMEM((48, 256), F32),
             pltpu.VMEM((CHUNK, 256), F32),
             pltpu.VMEM((288, 256), F32),
-            pltpu.VMEM((8, 4, 9, 128), F32),
+            pltpu.VMEM((9, 16, 256), F32),
             pltpu.VMEM((4, 9, 8, 128), F32),
-            pltpu.VMEM((4, 40, 128), F32),
-            pltpu.VMEM((4, 40, 128), F32),
-            pltpu.VMEM((8, 40, 512), F32),
+            pltpu.VMEM((8, 4, 40, 128), F32),
             pltpu.VMEM((1280, 256), F32),
-            DMA((4,)), DMA((4,)), DMA((8,)), DMA((8,)), DMA((8,)), DMA((8,)), DMA((4,)), DMA((4,)),
-            DMA((4,)), DMA((4,)), DMA((4,)), DMA((4,)), DMA((2,)),
+            DMA((32,)), DMA((32,)), DMA((32,)), DMA((32,)),
+            DMA((4, 4)), DMA((4, 4)), DMA((4, 4)), DMA((4, 4)),
         ],
         compiler_params=pltpu.CompilerParams(
             collective_id=1, has_side_effects=True, vmem_limit_bytes=48 * MIB
         ),
         name="window",
-    )(brief, params, consts, ids, listed, target, wide, tall, mix)
-
-
-def slots_of(entries):
-    _cell, _view, z, y, _x, _core = place()
-    owner = entries >> 7
-    dz = (z - (owner >> 2)) & 7
-    dy = (y - (owner & 3)) & 3
-    who = (((dy + dz) & 3) << 1) | (dz & 1)
-    return (((who << 2) | (dz >> 1)) << 7) | (entries & 127)
+    )(feat, params, consts, ids, listed, target, wide, tall, mix)
 
 
 def on_device(gaussians, cameras, fetch_ids, tile_lists, lengths, target_image):
     live = jnp.arange(512, dtype=jnp.int32)[:, None] < lengths[None, :]
-    listed = jnp.where(live, slots_of(tile_lists[0]).T, -1).reshape(1, 4096)
+    listed = jnp.where(live, tile_lists[0].T, -1).reshape(1, 4096)
     target = target_image.reshape(24, 256)
     ids, cams, table = ask(cameras, fetch_ids[0], gaussians)
-    brief, params, consts, mix = project(ids, cams, table)
-    picture, param_grads = window(brief, params, consts, ids, listed, target, mix)
+    feat, params, consts, mix = project(ids, cams, table)
+    picture, param_grads = window(feat, params, consts, ids, listed, target, mix)
     return picture.reshape(3, 1, 8, 256), param_grads
 
 

time: 75.5 us -> 72.2 us (0.956)
  Pallas kernels: 71 us -> 68 us
    pallas_call x1, Pallas kernels: 49.8 us -> 46.9 us  [window(): pl.pallas_call(window_kernel, out_shape=(shape(24, 256), shape(59, 4096))...]
where the time goes in v3:
time: 72.2 us; the launch traced here: 72.1 us
  Pallas kernels  68 us (94%)
  local copies, waits for them, and re-layouts  3.26 us (5%)
  between operations  0.73 us (1%)
    pallas_call x1, Pallas kernels, window(): pl.pallas_call(window_kernel, out_shape=(shape(24, 256), shape(59, 4096))...  46.9 us
    pallas_call x1, Pallas kernels, ask(): pl.pallas_call(ask_kernel, out_shape=(shape(4, 128, dtype=jnp.int32), sha...  15.5 us
    pallas_call x1, Pallas kernels, project(): pl.pallas_call(project_kernel, out_shape=(shape(4, 9, 8, 128), shape(4, 1...  5.66 us
    unnamed x16, local copies, waits for them, and re-layouts  2.97 us

profile of v3, /device:TPU:1, one launch (start us, length us, event | category | flops | bytes accessed | tf_op | source)
XLA Modules:
  0.0 72.1 jit_solution(15382644110094560732)
XLA Ops:
  0.6 0.0 copy-start.1
  0.6 0.7 copy-done.1
  1.4 0.0 copy-start.4
  1.4 0.7 copy-done.4
  2.0 0.0 copy-start.5
  2.0 0.0 copy-start.6
  2.0 0.0 copy-start
  2.0 0.0 copy-start.2
  2.0 0.0 copy-start.3
  2.0 15.5 %ask.1 = (s32[4,128]{1,0:T(4,128)S(1)}, f32[8,128]{1,0:T(8,128)S(1)}, f32[59,32768]{1,0:T(8,128)S(1)}) custom-call(f32[1,7]{1,0:T(1,128)S(1)} %copy-done.4, s32[32,128]{1,0:T(8,128)S(1)} %bitcast.11, f32[59,32768]{1,0:T(8,128)} %gauss_ref.1), custom_call_target="tpu_custom_call" | custom-call | tf_op jit(solution)/shard_map/ask/pallas_call | solution.py:673
  17.5 5.7 %project.1 = (f32[4,9,8,128]{3,2,1,0:T(8,128)S(1)}, f32[4,16,128]{2,1,0:T(8,128)S(1)}, f32[8,128]{1,0:T(8,128)S(1)}, f32[40,128]{1,0:T(8,128)S(1)}) custom-call(s32[4,128]{1,0:T(4,128)S(1)} %get-tuple-element.11.ids_ref, f32[8,128]{1,0:T(8,128)S(1)} %get-tuple-element.12.cams_ref, f32[59,32768]{1,0:T(8,128)S(1)} %get-tuple-element.13.tab), custom_call_target="tpu_custom_call" | custom-call | tf_op jit(solution)/shard_map/project/pallas_call | solution.py:693
  23.2 0.0 copy-done.5
  23.2 0.0 copy-done.6
  23.2 0.1 bitcast_select_fusion
  23.3 0.1 copy.12
  23.4 0.2 reshape.14.list_ref
  23.6 0.0 copy-done
  23.6 0.0 copy-done.2
  23.6 0.0 copy-done.3
  23.6 46.9 %window.1 = (f32[24,256]{1,0:T(8,128)S(1)}, f32[59,4096]{1,0:T(8,128)S(1)}) custom-call(f32[4,9,8,128]{3,2,1,0:T(8,128)S(1)} %get-tuple-element.14.feat_ref, f32[4,16,128]{2,1,0:T(8,128)S(1)} %get-tuple-element.15.params_ref, f32[8,128]{1,0:T(8,128)S(1)} %get-tuple-element.16.consts_ref, s32[4,128]{1,0:T(4,128)S(1)} %get-tuple-element.11.ids_ref, ...), custom_call_target="tpu_custom_call" | custom-call | tf_op jit(solution)/shard_map/window/pallas_call | solution.py:706
  70.5 0.6 copy.16
  71.1 1.0 %copy.17 = f32[59,4096]{1,0:T(8,128)} copy(f32[59,4096]{1,0:T(8,128)S(1)} %get-tuple-element.27) | data formatting | bytes 1933312
Async XLA Ops:
  0.6 0.7 copy-start.1
  1.4 0.7 copy-start.4
  2.0 21.2 %copy-start.5 = (s32[1,8,512]{2,1,0:T(8,128)S(1)}, s32[1,8,512]{2,1,0:T(8,128)}, u32[]{:S(2)}) copy-start(s32[1,8,512]{2,1,0:T(8,128)} %param.11) | copy-start | bytes 49156
  2.0 21.2 %copy-start.6 = (s32[8]{0:T(128)S(1)}, s32[8]{0:T(128)}, u32[]{:S(2)}) copy-start(s32[8]{0:T(128)} %param.12) | copy-start | bytes 100
  2.0 21.6 %copy-start = (f32[3,1,8,256]{3,2,1,0:T(8,128)S(1)}, f32[3,1,8,256]{3,2,1,0:T(8,128)}, u32[]{:S(2)}) copy-start(f32[3,1,8,256]{3,2,1,0:T(8,128)} %param.13) | copy-start | bytes 73732
  2.0 21.6 %copy-start.2 = (bf16[32,256]{1,0:T(8,128)(2,1)S(1)}, bf16[32,256]{1,0:T(8,128)(2,1)}, u32[]{:S(2)}) copy-start(bf16[32,256]{1,0:T(8,128)(2,1)} %constant.6.clone.basis_ref) | copy-start | bytes 49156
  2.0 21.6 %copy-start.3 = (bf16[16,256]{1,0:T(8,128)(2,1)S(1)}, bf16[16,256]{1,0:T(8,128)(2,1)}, u32[]{:S(2)}) copy-start(bf16[16,256]{1,0:T(8,128)(2,1)} %constant.7.clone.basis_t_ref) | copy-start | bytes 24580

commit v4 on v3

--- a/solution.py
+++ b/solution.py
@@ -423,13 +423,10 @@
             grad_chunk[8 * j:8 * j + 8, :] = jnp.where(seen < 0.99, weight[at, :] * gain, 0.0)
             behind = behind * (1.0 - seen) + seen * value[8 * j:8 * j + 8]
         grad = grad_chunk[...]
-        high, middle, low = three(grad)
+        high = grad.astype(BF16)
+        middle = (grad - high.astype(F32)).astype(BF16)
         basis_t = basis_t_ref[...]
-        moments = (
-            dot_nt(basis_t, high.astype(BF16))
-            + dot_nt(basis_t, middle.astype(BF16))
-            + dot_nt(basis_t, low.astype(BF16))
-        )
+        moments = dot_nt(basis_t, high) + dot_nt(basis_t, middle)
         tinted = dot_nt(wrong_w, weight_h[cols, :]) + dot_nt(wrong_w, weight_m[cols, :])
         tinted = tinted[0:24] + tinted[24:48]
         colour = [
@@ -515,6 +512,9 @@
 
     for n in range(32):
         grad_copy(n).start()
+    for i in range(4):
+        for v in range(8):
+            feature_copy(i, v).wait_send()
     acc[...] = jnp.zeros_like(acc)
 
     def far(step, i):
@@ -619,6 +619,8 @@
         acc[...] += dot_nt(jnp.concatenate(spread, axis=0), hot)
 
     deposit(view)
+    for n in range(32):
+        grad_copy(n).wait_send()
     for i in order:
         far_came(1, i)
         far_came(3, i)
@@ -627,6 +629,10 @@
         far_came(2, i)
     for step in (1, 3, 2):
         deposit((view - 2 * step) & 7)
+    for i in range(4):
+        for step in (1, 2, 3):
+            far(step, i).wait_send()
+        near(0, i).wait_send()
     for step in (1, 3, 2):
         deposit(near_came(step))
 
@@ -638,14 +644,7 @@
             precision=lax.Precision.HIGHEST, preferred_element_type=F32,
         )
     for i in range(4):
-        for v in range(8):
-            feature_copy(i, v).wait_send()
-    for n in range(32):
-        grad_copy(n).wait_send()
-    for i in range(4):
-        for step in (1, 2, 3):
-            far(step, i).wait_send()
-        for step in range(4):
+        for step in (1, 3, 2):
             near(step, i).wait_send()
 
 

time: 72.2 us -> 71.7 us (level)
  no operation moved by 1% of the time
where the time goes in v4:
time: 71.7 us; the launch traced here: 71.5 us
  Pallas kernels  67.5 us (94%)
  local copies, waits for them, and re-layouts  3.26 us (5%)
  between operations  0.73 us (1%)
    pallas_call x1, Pallas kernels, window(): pl.pallas_call(window_kernel, out_shape=(shape(24, 256), shape(59, 4096))...  46.3 us
    pallas_call x1, Pallas kernels, ask(): pl.pallas_call(ask_kernel, out_shape=(shape(4, 128, dtype=jnp.int32), sha...  15.5 us
    pallas_call x1, Pallas kernels, project(): pl.pallas_call(project_kernel, out_shape=(shape(4, 9, 8, 128), shape(4, 1...  5.66 us
    unnamed x16, local copies, waits for them, and re-layouts  2.97 us

profile of v4, /device:TPU:1, one launch (start us, length us, event | category | flops | bytes accessed | tf_op | source)
XLA Modules:
  0.0 71.5 jit_solution(6675227083564325551)
XLA Ops:
  0.6 0.0 copy-start.1
  0.6 0.7 copy-done.1
  1.4 0.0 copy-start.4
  1.4 0.7 copy-done.4
  2.0 0.0 copy-start.5
  2.0 0.0 copy-start.6
  2.0 0.0 copy-start
  2.0 0.0 copy-start.2
  2.0 0.0 copy-start.3
  2.0 15.5 %ask.1 = (s32[4,128]{1,0:T(4,128)S(1)}, f32[8,128]{1,0:T(8,128)S(1)}, f32[59,32768]{1,0:T(8,128)S(1)}) custom-call(f32[1,7]{1,0:T(1,128)S(1)} %copy-done.4, s32[32,128]{1,0:T(8,128)S(1)} %bitcast.11, f32[59,32768]{1,0:T(8,128)} %gauss_ref.1), custom_call_target="tpu_custom_call" | custom-call | tf_op jit(solution)/shard_map/ask/pallas_call | solution.py:672
  17.5 5.7 %project.1 = (f32[4,9,8,128]{3,2,1,0:T(8,128)S(1)}, f32[4,16,128]{2,1,0:T(8,128)S(1)}, f32[8,128]{1,0:T(8,128)S(1)}, f32[40,128]{1,0:T(8,128)S(1)}) custom-call(s32[4,128]{1,0:T(4,128)S(1)} %get-tuple-element.11.ids_ref, f32[8,128]{1,0:T(8,128)S(1)} %get-tuple-element.12.cams_ref, f32[59,32768]{1,0:T(8,128)S(1)} %get-tuple-element.13.tab), custom_call_target="tpu_custom_call" | custom-call | tf_op jit(solution)/shard_map/project/pallas_call | solution.py:692
  23.2 0.0 copy-done.5
  23.2 0.0 copy-done.6
  23.2 0.1 bitcast_select_fusion
  23.3 0.1 copy.12
  23.4 0.2 reshape.14.list_ref
  23.6 0.0 copy-done
  23.6 0.0 copy-done.2
  23.6 0.0 copy-done.3
  23.6 46.3 %window.1 = (f32[24,256]{1,0:T(8,128)S(1)}, f32[59,4096]{1,0:T(8,128)S(1)}) custom-call(f32[4,9,8,128]{3,2,1,0:T(8,128)S(1)} %get-tuple-element.14.feat_ref, f32[4,16,128]{2,1,0:T(8,128)S(1)} %get-tuple-element.15.params_ref, f32[8,128]{1,0:T(8,128)S(1)} %get-tuple-element.16.consts_ref, s32[4,128]{1,0:T(4,128)S(1)} %get-tuple-element.11.ids_ref, ...), custom_call_target="tpu_custom_call" | custom-call | tf_op jit(solution)/shard_map/window/pallas_call | solution.py:705
  70.0 0.6 copy.16
  70.6 1.0 %copy.17 = f32[59,4096]{1,0:T(8,128)} copy(f32[59,4096]{1,0:T(8,128)S(1)} %get-tuple-element.27) | data formatting | bytes 1933312
Async XLA Ops:
  0.6 0.7 %copy-start.1 = (s32[1,32,128]{2,1,0:T(8,128)S(1)}, s32[1,32,128]{2,1,0:T(8,128)}, u32[]{:S(2)}) copy-start(s32[1,32,128]{2,1,0:T(8,128)} %param.10) | copy-start | bytes 49156
  1.4 0.7 copy-start.4
  2.0 21.2 %copy-start.5 = (s32[1,8,512]{2,1,0:T(8,128)S(1)}, s32[1,8,512]{2,1,0:T(8,128)}, u32[]{:S(2)}) copy-start(s32[1,8,512]{2,1,0:T(8,128)} %param.11) | copy-start | bytes 49156
  2.0 21.2 %copy-start.6 = (s32[8]{0:T(128)S(1)}, s32[8]{0:T(128)}, u32[]{:S(2)}) copy-start(s32[8]{0:T(128)} %param.12) | copy-start | bytes 100
  2.0 21.6 %copy-start = (f32[3,1,8,256]{3,2,1,0:T(8,128)S(1)}, f32[3,1,8,256]{3,2,1,0:T(8,128)}, u32[]{:S(2)}) copy-start(f32[3,1,8,256]{3,2,1,0:T(8,128)} %param.13) | copy-start | bytes 73732
  2.0 21.6 %copy-start.2 = (bf16[32,256]{1,0:T(8,128)(2,1)S(1)}, bf16[32,256]{1,0:T(8,128)(2,1)}, u32[]{:S(2)}) copy-start(bf16[32,256]{1,0:T(8,128)(2,1)} %constant.6.clone.basis_ref) | copy-start | bytes 49156
  2.0 21.6 %copy-start.3 = (bf16[16,256]{1,0:T(8,128)(2,1)S(1)}, bf16[16,256]{1,0:T(8,128)(2,1)}, u32[]{:S(2)}) copy-start(bf16[16,256]{1,0:T(8,128)(2,1)} %constant.7.clone.basis_t_ref) | copy-start | bytes 24580
